TPU v7x, 32 devices: a whole 2x2x4 slice. The times are simulated.
32 devices in a mesh: space: 2 (over x), mrow: 4 (over y, core), mcol: 4 (over z).
Axes of the slice: x: 2, y: 2, z: 4, core: 2. Of those that a mesh axis runs over, the one named last changes fastest.
Arguments:
- deviation: bfloat16 [64, 48, 8192], P('space', None, ('mcol', 'mrow'))
- courant: float32 [2, 8192], P(None, ('mcol', 'mrow')), may hold values from -0.95 to 0.95
- collide: bfloat16 [8192, 8192], P('mrow', ('mcol', 'space'))
- hole_cells: int32 [768], P('space'), may hold values from -1 to 1535, as said below
- hole_wall: int32 [768], P('space'), may hold values from 0 to 3
- specular: int32 [4, 8192], replicated, may hold values from 0 to 8191, as said below
- specularity: float32 [4], replicated, may hold values from 0.2 to 0.8
Outputs:
- updated: bfloat16 [64, 48, 8192], P('space', None, ('mrow', 'mcol'))
Inputs may be any that keep to these rules, and one draw needn't show every extreme that they name: `hole_cells`: within one tile the used slots come first and name distinct cells; every tile has at least 96 used slots, some tile has all 384 slots used and some tile has an empty slot. Each row specular[w] is a permutation of the modes; for an outgoing mode i of aligned block e = i // 512, its incoming mode j lies, within j's own aligned block of 512 modes, in the sub-block of 32 modes numbered e, that is (j % 512) // 32 == e.
All inputs are finite; a program needn't handle non-finite values.
Results may differ from a plain program's by a relative error of at most 0.005.
Values may be sent and summed in bfloat16 or wider, within the bound.
No kernel may reach another device: no remote copies, remote signals or barrier semaphores. Data moves between devices by JAX's collectives and lax.ppermute only.
A program may use at most 128 MiB of HBM per device.

v0:
```python
import functools
import jax
import jax.numpy as jnp
import numpy as np
from jax import lax
from jax.experimental import pallas as pl
from jax.experimental.pallas import tpu as pltpu
from jax.sharding import PartitionSpec as P

SMEM = pltpu.SMEM
HBM = pltpu.HBM
NT = (((1,), (1,)), ((), ()))
SPLIT = (2, 1)
LIMIT = 60 * 1024 * 1024
HOP_LIMIT = 16 * 1024 * 1024


def takes(microseconds):
    return pl.CostEstimate(flops=int(microseconds * 0.5e9), bytes_accessed=0, transcendentals=0)


TAIL = 16


def line_steps(size):
    order = []
    for c in range(size):
        row = []
        for t in range(1, size):
            if c <= t - 1:
                row.append(c + size - t)
            if c >= size - t:
                row.append(c - size + t)
        row.append(c)
        order.append(row)
    return np.array(order, np.int32)


def slot_of(c, t, size):
    place = 0
    for u in range(1, t):
        place = place + jnp.where(c <= u - 1, 1, 0) + jnp.where(c >= size - u, 1, 0)
    return place


def slots_at(t, size):
    found = set()
    for c in range(size):
        place = 0
        for u in range(1, size):
            for hit in (c <= u - 1, c >= size - u):
                if hit:
                    if u == t:
                        found.add(place)
                    place += 1
        if t == size:
            found.add(size - 1)
    return sorted(found)


def moves(lane, head, fill, spare, on_rim):
    slots = lane.shape[1]
    sub = jnp.broadcast_to(lane, (128, slots)).T[:, 0:1]
    total = jnp.sum((lane >= 0).astype(jnp.float32), axis=1, keepdims=True).astype(jnp.int32)
    in_head = jnp.logical_and(lane >= 0, lane < head)
    head_count = jnp.sum(in_head.astype(jnp.float32), axis=1, keepdims=True).astype(jnp.int32)
    place = lax.broadcasted_iota(jnp.int32, (1, slots), 1)
    tail = jnp.broadcast_to(place + head, (slots, slots))
    wide_sub = jnp.broadcast_to(sub, (slots, slots))
    before = jnp.logical_and(wide_sub >= head, wide_sub < tail).astype(jnp.float32)
    hit = (wide_sub == tail).astype(jnp.float32)
    rank = place - jnp.sum(before, axis=0, keepdims=True).astype(jnp.int32)
    tail_key = jnp.where(jnp.sum(hit, axis=0, keepdims=True) > 0, -2, rank)
    row = lax.broadcasted_iota(jnp.int32, (head, slots), 0)
    wide_lane = jnp.broadcast_to(lane, (head, slots))
    ahead = jnp.logical_and(wide_lane >= 0, wide_lane < row).astype(jnp.float32)
    hits = jnp.max((wide_lane == row).astype(jnp.float32), axis=1, keepdims=True)
    head_key = jnp.where(hits > 0, jnp.sum(ahead, axis=1, keepdims=True).astype(jnp.int32), -1)
    on_rim[...] = hits
    fill[...] = (head_key == tail_key).astype(jnp.float32).astype(jnp.bfloat16)
    slot = lax.broadcasted_iota(jnp.int32, (slots, 1), 0)
    slot_key = jnp.where(slot >= total, slot - total + head_count, -1)
    spare[...] = (slot_key == tail_key).astype(jnp.float32).astype(jnp.bfloat16)
    return sub


def late_mask_kernel(
    rows_of, cols_of, cells_lane, table, mirror, place, spare, fill, fill_more, on_rim, on_rim_more, fills, flags
):
    cell = lax.broadcasted_iota(jnp.int32, place.shape, 0)
    place[...] = (cells_lane[...] == cell).astype(jnp.float32).astype(jnp.bfloat16)
    modes = mirror.shape[1]
    piece = modes // (rows_of * cols_of)
    entry = table[...]
    block = lax.div(entry, modes)
    group = lax.rem(block, rows_of) * cols_of + lax.div(block, rows_of)
    position = group * piece + lax.rem(entry, piece)
    source = lax.broadcasted_iota(jnp.int32, mirror.shape[1:], 0)
    for w in range(mirror.shape[0]):
        mirror[w] = (position[w : w + 1] == source).astype(jnp.float32).astype(jnp.bfloat16)
    moves(cells_lane[...], fills.shape[0], fills, spare, flags)
    kept = fill.shape[0]
    fill[...] = fills[:kept, :]
    fill_more[...] = fills[kept:, :]
    on_rim[...] = flags[:kept, :]
    on_rim_more[...] = flags[kept:, :]


def read_kernel(count, shards, *refs):
    refs = list(refs)
    where, dev, courant, cells_lane = (refs.pop(0) for _ in range(4))
    edges = [refs.pop(0) for _ in range(2 if not shards else 1)]
    table, whole = (refs.pop(0) for _ in range(2)) if shards else (None, None)
    extra = refs.pop(0)
    outs = [refs.pop(0) for _ in range(count)]
    parts = [refs.pop(0) for _ in range(shards)]
    read, fill, spare, on_rim = (refs.pop(0) for _ in range(4))
    fetches, stores = [], []
    if shards:
        stage, in_sem, out_sem = refs
        rows = stage.shape[1]
        for j in range(shards):
            first = pl.multiple_of(table[where[2], j] * rows, rows)
            fetches.append(
                pltpu.make_async_copy(whole.at[pl.ds(first, rows), :], stage.at[j], in_sem.at[j])
            )
            stores.append(pltpu.make_async_copy(stage.at[j], parts[j], out_sem.at[j]))
    for copy in fetches:
        copy.start()
    moves(cells_lane[...], fill.shape[0], fill, spare, on_rim)
    width_x, width_y, modes = dev.shape
    speed = courant[...]
    reach = jnp.abs(speed)
    ahead = jnp.where(speed > 0, 1.0, 0.0)
    if shards:
        edge = edges[0][0].astype(jnp.float32)
        before, after = jnp.where(where[0] == 1, edge, 0.0), jnp.where(where[0] == 0, edge, 0.0)
    else:
        before, after = edges[0][0].astype(jnp.float32), edges[1][0].astype(jnp.float32)
    lanes = 128
    moving = list(zip(fetches, stores))
    for low in range(0, modes, lanes):
        if low and moving:
            fetch, store = moving.pop(0)
            fetch.wait()
            store.start()
        cut = slice(low, low + lanes)
        a, b = reach[0:1, cut], reach[1:2, cut]
        stay_x, stay_y = 1.0 - a, 1.0 - b
        ahead_x = jnp.broadcast_to(ahead[0:1, cut], (width_y, lanes)) > 0
        ahead_y = jnp.broadcast_to(ahead[1:2, cut], (width_y, lanes)) > 0

        def one(x, behind, center, beyond):
            along = stay_x * center + a * jnp.where(ahead_x, behind, beyond)
            shifted = jnp.where(ahead_y, pltpu.roll(along, 1, 0), pltpu.roll(along, width_y - 1, 0))
            value = stay_y * along + b * shifted
            read[pl.ds(pl.multiple_of(x * width_y, 16), width_y), cut] = value.astype(read.dtype)

        def body(x, carry):
            behind, center = carry
            beyond = dev[x + 1, :, cut].astype(jnp.float32)
            one(x, behind, center, beyond)
            return center, beyond

        carry = (before[:, cut], dev[0, :, cut].astype(jnp.float32))
        behind, center = lax.fori_loop(0, width_x - 1, body, carry, unroll=4)
        one(width_x - 1, behind, center, after[:, cut])

    for fetch, store in moving:
        fetch.wait()
        store.start()
    head = read.shape[0] - extra.shape[0]
    tail_rows = read[head:, :]
    first = 0
    for out in outs:
        rows = slice(first, first + out.shape[0])
        first += out.shape[0]
        moved = jnp.dot(fill[rows, :], tail_rows, preferred_element_type=jnp.float32)
        kept = read[rows, :].astype(jnp.float32)
        out[...] = jnp.where(on_rim[rows, :] > 0, moved, kept).astype(out.dtype)
    extra[...] = jnp.dot(spare[...], tail_rows, preferred_element_type=jnp.float32).astype(extra.dtype)

    for store in stores:
        store.wait()


def payload_kernel(rows_of, cols_of, cells_lane, read, payload):
    slots, modes = payload.shape[2], read.shape[1]
    sub = jnp.broadcast_to(cells_lane[...], (128, slots)).T[:, 0:1]
    cell = lax.broadcasted_iota(jnp.int32, (slots, read.shape[0]), 1)
    select = (sub == cell).astype(jnp.float32).astype(jnp.bfloat16)
    rim = jnp.dot(select, read[...], preferred_element_type=jnp.float32)
    flipped = rim.T
    total = jnp.sum(flipped, axis=0, keepdims=True)
    high = total.astype(jnp.bfloat16).astype(jnp.float32)
    middle = (total - high).astype(jnp.bfloat16).astype(jnp.float32)
    low = total - high - middle
    place = lax.broadcasted_iota(jnp.int32, (TAIL, total.shape[1]), 0)
    tail = jnp.where(place == 0, high, jnp.where(place == 1, middle, jnp.where(place == 2, low, 0.0)))
    tail = tail.astype(jnp.bfloat16)
    piece = modes // (rows_of * cols_of)
    packed = flipped.astype(jnp.bfloat16)
    for r in range(rows_of):
        for c in range(cols_of):
            block = c * rows_of + r
            payload[r * cols_of + c, 0:piece, :] = packed[block * piece : (block + 1) * piece]
            payload[r * cols_of + c, piece : piece + TAIL, :] = tail


def rim_kernel(mode_count, specularity, arrived, mirror, wall, cells_lane, extra, out):
    groups, height, slots = arrived.shape
    piece = height - TAIL
    values = arrived[:, 0:piece, :].reshape(groups * piece, slots).T
    sums = arrived[:, piece:height, :].reshape(groups * TAIL, slots).astype(jnp.float32)
    total = jnp.broadcast_to(jnp.sum(sums, axis=0, keepdims=True), (128, slots)).T
    diffuse = total[:, 0:1] / mode_count
    walls = jnp.broadcast_to(wall[...], (128, slots)).T[:, 0:1]
    share = jnp.zeros(walls.shape, jnp.float32)
    mirrored = jnp.zeros(out.shape, jnp.float32)
    for w in range(mirror.shape[0]):
        share = jnp.where(walls == w, specularity[w], share)
        picked = jnp.dot(values, mirror[w], preferred_element_type=jnp.float32)
        mirrored = jnp.where(walls == w, picked, mirrored)
    emitted = share * mirrored + (1.0 - share) * diffuse
    used = jnp.broadcast_to(cells_lane[...], (128, slots)).T[:, 0:1] >= 0
    out[...] = jnp.where(used, emitted, extra[...].astype(jnp.float32)).astype(out.dtype)


def base_kernel(fill, on_rim, part, base):
    kept = part.shape[0]
    base[:kept, :] = jnp.where(on_rim[...] > 0, 0.0, part[...].astype(jnp.float32)).astype(base.dtype)
    moved = lax.dot_general(
        fill[...], part[...], (((0,), (0,)), ((), ())), preferred_element_type=jnp.float32
    )
    base[kept:, :] = moved.astype(base.dtype)


def merge_kernel(fill, spare, place, on_rim, base, total, from_left, from_right, out):
    slots = spare.shape[0]
    kept = base.shape[0] - slots
    total = total[...] + from_left[...].astype(jnp.float32) + from_right[...].astype(jnp.float32)
    total = total.astype(jnp.bfloat16)
    more = total.shape[0] - slots
    part, last = total[:more, :], total[more:, :]
    head = kept + more
    tn = (((0,), (0,)), ((), ()))
    moved = jnp.dot(place[:kept, :], last, preferred_element_type=jnp.float32)
    out[:kept, :] = (base[:kept, :].astype(jnp.float32) + moved).astype(out.dtype)
    moved = jnp.dot(place[kept:head, :], last, preferred_element_type=jnp.float32)
    out[kept:head, :] = jnp.where(on_rim[...] > 0, moved, part.astype(jnp.float32)).astype(out.dtype)
    moved = jnp.dot(place[head:, :], last, preferred_element_type=jnp.float32)
    moved = moved + lax.dot_general(spare[...], last, tn, preferred_element_type=jnp.float32)
    moved = moved + lax.dot_general(fill[...], part, tn, preferred_element_type=jnp.float32)
    out[head:, :] = (base[kept:, :].astype(jnp.float32) + moved).astype(out.dtype)


def hop_kernel(t, size, wide, slots, groups, has_recv, *refs):
    refs = list(refs)
    where = refs.pop(0)
    blocks = [[refs.pop(0) for _ in range(4)] for _ in range(groups)]
    own = refs.pop(0) if wide else None
    held = {j: (refs.pop(0), refs.pop(0)) for j in slots}
    final = t == size
    recv = [refs.pop(0), refs.pop(0)] if has_recv else None
    outs = [refs.pop(0)] if final else [refs.pop(0), refs.pop(0)]
    buffer, sem = refs
    s, r, c = where[0], where[1], where[2]
    rows = buffer.shape[1]
    width = blocks[0][0].shape[1]
    if final:
        jobs = [(c, None, size - 1)]
    else:
        first = slot_of(c, t, size)
        goes_right = c <= t - 1
        jobs = [
            (c + size - t, goes_right, first),
            (c - size + t, c >= size - t, first + jnp.where(goes_right, 1, 0)),
        ]

    def fetch(n, d, place):
        for b in range(4):
            source = lax.bitwise_xor(r, b)
            target = buffer.at[n, :, b * width : (b + 1) * width]
            if wide:
                column = pl.multiple_of(source * width, width)
                pltpu.make_async_copy(
                    own.at[pl.ds(pl.multiple_of(d * rows, rows), rows), pl.ds(column, width)],
                    target,
                    sem.at[n],
                ).start()
                continue
            column = pl.multiple_of(lax.bitwise_and(source, 1) * width, width)
            is_own = lax.shift_right_logical(source, 1) == s
            for j, pair in held.items():
                for use, shard in ((is_own, pair[0]), (jnp.logical_not(is_own), pair[1])):

                    @pl.when(jnp.logical_and(use, place == j))
                    def _(shard=shard):
                        pltpu.make_async_copy(shard.at[:, pl.ds(column, width)], target, sem.at[n]).start()

    def multiply(n, out):
        pltpu.make_async_copy(buffer.at[n], buffer.at[n], sem.at[n]).wait()
        first = 0
        for group in blocks:
            height = group[0].shape[0]
            tile = min(384, height)

            def rows_of_tile(i, carry, group=group, first=first, tile=tile):
                low = pl.multiple_of(i * tile, tile)
                inside, rows_here = pl.ds(low, tile), pl.ds(first + low, tile)
                total = None
                for b in range(4):
                    part = lax.dot_general(
                        group[b][inside, :],
                        buffer[n, :, b * width : (b + 1) * width],
                        NT,
                        preferred_element_type=jnp.float32,
                    )
                    total = part if total is None else total + part
                if final and has_recv:
                    total = total + recv[0][rows_here, :].astype(jnp.float32)
                    total = total + recv[1][rows_here, :].astype(jnp.float32)
                elif has_recv:
                    total = total + recv[n][rows_here, :].astype(jnp.float32)
                out[rows_here, :] = total.astype(out.dtype)
                return carry

            lax.fori_loop(0, height // tile, rows_of_tile, 0)
            first += height

    for n, (d, valid, place) in enumerate(jobs):
        if valid is None:
            fetch(n, d, place)
        else:
            pl.when(valid)(functools.partial(fetch, n, d, place))
    for n, (d, valid, place) in enumerate(jobs):
        if valid is None:
            multiply(n, outs[n])
        else:
            pl.when(valid)(functools.partial(multiply, n, outs[n]))


def hop(t, size, where, blocks, own, held, recv):
    wide = own is not None
    slots = () if wide else tuple(slots_at(t, size))
    rows = own.shape[0] // size if wide else held[0][0].shape[0]
    cells = sum(group[0].shape[0] for group in blocks)
    width = blocks[0][0].shape[1]
    count = 1 if t == size else 2
    kept = jnp.float32 if t == size and recv is None else jnp.bfloat16
    spec = pl.BlockSpec(memory_space=pltpu.VMEM)
    any_spec = pl.BlockSpec(memory_space=HBM)
    shards = [own] if wide else [shard for j in slots for shard in held[j]]
    operands = [where, *[block for group in blocks for block in group], *shards, *(recv or [])]
    in_specs = [pl.BlockSpec(memory_space=SMEM)] + [spec] * (4 * len(blocks)) + [any_spec] * len(shards)
    in_specs += [spec] * len(recv or [])
    return pl.pallas_call(
        functools.partial(hop_kernel, t, size, wide, slots, len(blocks), recv is not None),
        out_shape=[jax.ShapeDtypeStruct((cells, rows), kept)] * count,
        in_specs=in_specs,
        out_specs=[spec] * count,
        scratch_shapes=[
            pltpu.VMEM((count, rows, 4 * width), jnp.bfloat16),
            pltpu.SemaphoreType.DMA((count,)),
        ],
        compiler_params=pltpu.CompilerParams(vmem_limit_bytes=HOP_LIMIT),
        cost_estimate=takes(2 + cells / 300),
    )(*operands)


def on_device(deviation, courant, collide, hole_cells, hole_wall, specular, specularity):
    n_space, n_row, n_col = (lax.axis_size(name) for name in ("space", "mrow", "mcol"))
    s, r, c = (lax.axis_index(name) for name in ("space", "mrow", "mcol"))
    width_x, width_y, block_len = deviation.shape
    cell_count = width_x * width_y
    slot_count = hole_cells.shape[0]
    wall_count, mode_count = specular.shape
    piece = block_len // (n_row * n_col)
    groups = n_row * n_col
    vmem = pl.BlockSpec()
    hbm = pl.BlockSpec(memory_space=HBM)
    smem = pl.BlockSpec(memory_space=SMEM)
    params = pltpu.CompilerParams(vmem_limit_bytes=LIMIT)
    roomy = pltpu.CompilerParams(vmem_limit_bytes=24 * 1024 * 1024)
    where = jnp.stack([s, r, c]).astype(jnp.int32)

    if n_space == 2:
        edge = jnp.where(s == 0, deviation[-1:], deviation[:1])
        edges = [lax.ppermute(edge, "space", [(0, 1), (1, 0)])]
    else:
        up = [(i, i + 1) for i in range(n_space - 1)]
        down = [(j, i) for i, j in up]
        edges = [lax.ppermute(deviation[-1:], "space", up), lax.ppermute(deviation[:1], "space", down)]

    def after(value, *first):
        return lax.optimization_barrier((value, first))[0]

    def shape(*dims):
        return jax.ShapeDtypeStruct(dims, jnp.bfloat16)

    head = cell_count - slot_count
    sizes = [head * part // sum(SPLIT) for part in SPLIT]
    count = len(sizes)
    lane_cells = hole_cells[None, :]
    wide = n_space != 2
    rows = collide.shape[0] // n_col
    own = lax.all_gather(collide, "space", axis=1, tiled=True) if wide else None
    shards = 0 if wide else n_col
    swap = [(0, 1), (1, 0)]
    held, order = [], jnp.asarray(line_steps(n_col))
    extra, *mine = pl.pallas_call(
        functools.partial(read_kernel, count, shards),
        out_shape=[shape(slot_count, block_len)]
        + [shape(size, block_len) for size in sizes]
        + [shape(rows, collide.shape[1])] * shards
        + [shape(cell_count, block_len)],
        in_specs=[smem] + [vmem] * (3 + len(edges)) + [smem, hbm][: shards * 2],
        out_specs=[vmem] * (count + 1) + [hbm] * shards + [vmem],
        scratch_shapes=[
            pltpu.VMEM((head, slot_count), jnp.bfloat16),
            pltpu.VMEM((slot_count, slot_count), jnp.bfloat16),
            pltpu.VMEM((head, 1), jnp.float32),
        ]
        + [
            pltpu.VMEM((shards, rows, collide.shape[1]), jnp.bfloat16),
            pltpu.SemaphoreType.DMA((shards,)),
            pltpu.SemaphoreType.DMA((shards,)),
        ][: shards * 3],
        compiler_params=params,
        cost_estimate=takes(6),
    )(where, deviation, courant, lane_cells, *edges, *([] if wide else [order, collide]))
    read = mine.pop()
    payload = pl.pallas_call(
        functools.partial(payload_kernel, n_row, n_col),
        out_shape=shape(groups, piece + TAIL, slot_count),
        in_specs=[vmem] * 2,
        out_specs=vmem,
        compiler_params=params,
        cost_estimate=takes(3),
    )(lane_cells, read)
    mine, parts = mine[:count], mine[count:]
    for part in parts:
        held.append((part, lax.ppermute(part, "space", swap)))

    flip = [[(i, i ^ bit) for i in range(n_row)] for bit in (1, 2)]
    right = [(i, i + 1) for i in range(n_col - 1)]
    left = [(j, i) for i, j in right]
    far = []
    for value in mine:
        far.append(lax.ppermute(value, "mrow", flip[1]))
    arrived = lax.all_to_all(payload, ("mrow", "mcol"), split_axis=0, concat_axis=0, tiled=True)
    def send(t, value):
        return [
            lax.ppermute(value[0], "mcol", right[:t]),
            lax.ppermute(value[1], "mcol", left[n_col - 1 - t :]),
        ]

    state = {}
    done = ()

    def step(t, n, *ready):
        return hop(t, n_col, after(where, *done, *ready), chunks[n], own, held, state.get(n))

    def gather(n):
        near = lax.ppermute(mine[n], "mrow", flip[0])
        both = lax.ppermute(after(far[n], *done), "mrow", flip[0])
        return [mine[n], near, far[n], both]

    own_table = lax.dynamic_slice_in_dim(specular, (c * n_row + r) * block_len, block_len, 1)
    mirror, place, spare, fill, fill_more, on_rim, on_rim_more = pl.pallas_call(
        functools.partial(late_mask_kernel, n_row, n_col),
        out_shape=[
            shape(wall_count, block_len, block_len),
            shape(cell_count, slot_count),
            shape(slot_count, slot_count),
            *[shape(size, slot_count) for size in sizes],
            *[jax.ShapeDtypeStruct((size, 1), jnp.float32) for size in sizes],
        ],
        in_specs=[vmem] * 2,
        out_specs=[vmem] * 7,
        scratch_shapes=[pltpu.VMEM((head, slot_count), jnp.bfloat16), pltpu.VMEM((head, 1), jnp.float32)],
        compiler_params=params,
        cost_estimate=takes(4),
    )(after(lane_cells, extra), own_table)
    far[0] = after(far[0], mirror, *[other for _, other in held[:1]])
    chunks = [[gather(0)]]
    done = step(1, 0, arrived)
    state[0] = send(1, done)
    mine.append(
        pl.pallas_call(
            functools.partial(rim_kernel, mode_count),
            out_shape=shape(slot_count, block_len),
            in_specs=[smem] + [vmem] * 5,
            out_specs=vmem,
            compiler_params=roomy,
            cost_estimate=takes(4),
        )(specularity, after(arrived, far[1], *done), mirror, hole_wall[None, :], lane_cells, extra)
    )
    far.append(lax.ppermute(mine[count], "mrow", flip[1]))
    chunks.append([gather(n) for n in range(1, count + 1)])
    done = step(1, 1, *state[0])
    state[1] = send(1, done)
    outs = []
    for t in range(2, n_col + 1):
        for n in (0, 1):
            if (t, n) == (n_col, 1):
                continue
            done = step(t, n)
            if t == n_col:
                outs.append(done[0])
            else:
                state[n] = send(t, done)
    total = hop(n_col, n_col, after(where, *done), chunks[1], own, held, None)[0]
    base = pl.pallas_call(
        base_kernel,
        out_shape=shape(sizes[0] + slot_count, rows),
        in_specs=[vmem] * 3,
        out_specs=vmem,
        compiler_params=roomy,
        cost_estimate=takes(2),
    )(fill, on_rim, *outs)
    near = pl.BlockSpec(memory_space=pltpu.VMEM)
    out = pl.pallas_call(
        merge_kernel,
        out_shape=shape(cell_count, rows),
        in_specs=[near] * 8,
        out_specs=vmem,
        compiler_params=pltpu.CompilerParams(vmem_limit_bytes=HOP_LIMIT),
        cost_estimate=takes(4),
    )(fill_more, spare, place, on_rim_more, base, total, *state[1])
    return out.reshape(width_x, width_y, rows)


def solution(mesh):
    in_specs = (
        P("space", None, ("mcol", "mrow")),
        P(None, ("mcol", "mrow")),
        P("mrow", ("mcol", "space")),
        P("space"),
        P("space"),
        P(),
        P(),
    )
    out_specs = P("space", None, ("mrow", "mcol"))
    return jax.shard_map(
        on_device, mesh=mesh, in_specs=in_specs, out_specs=out_specs, check_vma=False
    )
```

profile of v0, /device:TPU:20, one launch (start us, length us, event | category | flops | bytes accessed | tf_op | source)
XLA Modules:
  0.0 161.2 jit_solution(4963224691895866977)
XLA Ops:
  5.6 7.1 %shard_map.82 = (bf16[384,512]{1,0:T(8,128)(2,1)}, bf16[768,512]{1,0:T(8,128)(2,1)}, bf16[384,512]{1,0:T(8,128)(2,1)}, bf16[512,1024]{1,0:T(8,128)(2,1)}, bf16[5...) custom-call(s32[3]{0:T(128)} %pad_add_fusion.refs_0_, ...), custom_call_target="tpu_custom_call" | custom-call | flops 3000000000 | tf_op jit(solution)/shard_map/pallas_call | solution.py:411
  14.8 3.6 %shard_map.84 = bf16[16,48,384]{2,1,0:T(8,128)(2,1)} custom-call(s32[1,384]{1,0:T(1,128)} %broadcast_in_dim.6.refs_3_.cells_lane, bf16[1536,512]{1,0:T(8,128)(2,1)} %get-tuple-element.53.read), custom_call_target="tpu_custom_call" | custom-call | flops 1500000000 | tf_op jit(solution)/shard_map/pallas_call | solution.py:433
  18.3 6.2 %all-to-all-start = ((bf16[16,48,384]{2,1,0:T(8,128)(2,1)}), bf16[16,48,384]{2,1,0:T(8,128)(2,1)}, u32[]{:S(2)}, u32[]{:S(2)}) async-start(bf16[16,48,384]{2,1,0:T(8,128)(2,1)} %shard_map.84), calls=%async_computation | async-start | bytes 1179648 | tf_op jit(solution)/shard_map/all_to_all | solution.py:451
  25.3 4.6 %shard_map.83 = (bf16[4,512,512]{2,1,0:T(8,128)(2,1)}, bf16[1536,384]{1,0:T(8,128)(2,1)}, bf16[384,384]{1,0:T(8,128)(2,1)}, bf16[768,384]{1,0:T(8,128)(2,1)}, bf...) custom-call(s32[1,384]{1,0:T(1,128)} %broadcast_in_dim.6.refs_3_.cells_lane, ...), custom_call_target="tpu_custom_call" | custom-call | flops 2000000000 | tf_op jit(solution)/shard_map/pallas_call | solution.py:470
  29.9 7.9 %collective-permute-done.2.refs_3_ = bf16[768,512]{1,0:T(8,128)(2,1)} collective-permute-done((bf16[768,512]{1,0:T(8,128)(2,1)}, bf16[768,512]{1,0:T(8,128)(2,1)}, u32[]{:S(2)}, u32[]{:S(2)}) %collective-permute-start.2) | collective-permute-done | bytes 786464 | tf_op jit(solution)/shard_map/ppermute | solution.py:450
  38.4 2.0 %collective-permute-done.4.refs_4_ = bf16[768,512]{1,0:T(8,128)(2,1)} collective-permute-done((bf16[768,512]{1,0:T(8,128)(2,1)}, bf16[768,512]{1,0:T(8,128)(2,1)}, u32[]{:S(2)}, u32[]{:S(2)}) %collective-permute-start.4) | collective-permute-done | bytes 786464 | tf_op jit(solution)/shard_map/ppermute | solution.py:466
  40.4 1.7 %shard_map.85 = (bf16[768,512]{1,0:T(8,128)(2,1)S(1)}, bf16[768,512]{1,0:T(8,128)(2,1)S(1)}) custom-call(s32[3]{0:T(128)S(1)} %copy-done.10, bf16[768,512]{1,0:T(8,128)(2,1)S(1)} %copy-done.4, bf16[768,512]{1,0:T(8,128)(2,1)} %collective-permute-done.1.refs_2_, bf16[768,512]{1,0:T(8,128)(2,1)} %collective-permute-done.2.refs_3_, ...), custom_call_target="tpu_custom_call" | custom-call | flops 2280000000 | tf_op jit(solution)/shard_map/pallas_call | solution.py:357
  44.1 5.4 %collective-permute-done.8.refs_3_ = bf16[384,512]{1,0:T(8,128)(2,1)} collective-permute-done((bf16[384,512]{1,0:T(8,128)(2,1)S(1)}, bf16[384,512]{1,0:T(8,128)(2,1)}, u32[]{:S(2)}, u32[]{:S(2)}) %collective-permute-start.8) | collective-permute-done | bytes 393248 | tf_op jit(solution)/shard_map/ppermute | solution.py:450
  49.5 2.2 %shard_map.86.refs_5_ = bf16[384,512]{1,0:T(8,128)(2,1)S(1)} custom-call(f32[4]{0:T(128)S(1)} %copy-done.13, bf16[16,48,384]{2,1,0:T(8,128)(2,1)} %all-to-all-done.arrived, bf16[4,512,512]{2,1,0:T(8,128)(2,1)S(1)} %copy-done.16, s32[1,384]{1,0:T(1,128)S(1)} %broadcast_in_dim.7.wall, s32[1,384]{1,0:T(1,128)S(1)} %copy-done.11, bf16[384,512]{1,0:T(8,128)(2,1)S(1)} %copy-done.17), custom_call_target="tpu_custom_call" | custom-call | flops 2000000000 | tf_op jit(solution)/shard_map/pallas_call | solution.py:490
  53.0 9.5 %collective-permute-done.11.refs_7_ = bf16[384,512]{1,0:T(8,128)(2,1)S(1)} collective-permute-done((bf16[384,512]{1,0:T(8,128)(2,1)S(1)}, bf16[384,512]{1,0:T(8,128)(2,1)S(1)}, u32[]{:S(2)}, u32[]{:S(2)}) %collective-permute-start.11) | collective-permute-done | bytes 393248 | tf_op jit(solution)/shard_map/ppermute | solution.py:499
  63.1 3.0 %collective-permute-done.6.refs_10_ = bf16[768,512]{1,0:T(8,128)(2,1)S(1)} collective-permute-done((bf16[768,512]{1,0:T(8,128)(2,1)S(1)}, bf16[768,512]{1,0:T(8,128)(2,1)S(1)}, u32[]{:S(2)}, u32[]{:S(2)}) %collective-permute-start.6) | collective-permute-done | bytes 786464 | tf_op jit(solution)/shard_map/ppermute | solution.py:455
  66.0 1.7 %collective-permute-done.12.refs_8_ = bf16[384,512]{1,0:T(8,128)(2,1)S(1)} collective-permute-done((bf16[384,512]{1,0:T(8,128)(2,1)S(1)}, bf16[384,512]{1,0:T(8,128)(2,1)S(1)}, u32[]{:S(2)}, u32[]{:S(2)}) %collective-permute-start.12) | collective-permute-done | bytes 393248 | tf_op jit(solution)/shard_map/ppermute | solution.py:466
  71.8 6.4 %collective-permute-done.13.refs_8_.refs_12_.refs_6_.refs_10_ = bf16[512,1024]{1,0:T(8,128)(2,1)S(1)} collective-permute-done((bf16[512,1024]{1,0:T(8,128)(2,1)S(1)}, bf16[512,1024]{1,0:T(8,128)(2,1)S(1)}, u32[]{:S(2)}, u32[]{:S(2)}) %collective-permute-start.13) | collective-permute-done | bytes 1048608 | tf_op jit(solution)/shard_map/ppermute | solution.py:443
  78.2 4.1 %shard_map.88 = (bf16[768,512]{1,0:T(8,128)(2,1)S(1)}, bf16[768,512]{1,0:T(8,128)(2,1)S(1)}) custom-call(s32[3]{0:T(128)S(1)} %copy-done.10, bf16[768,512]{1,0:T(8,128)(2,1)S(1)} %copy-done.4, bf16[768,512]{1,0:T(8,128)(2,1)} %collective-permute-done.1.refs_2_, bf16[768,512]{1,0:T(8,128)(2,1)} %collective-permute-done.2.refs_3_, ...), custom_call_target="tpu_custom_call" | custom-call | flops 2280000000 | tf_op jit(solution)/shard_map/pallas_call | solution.py:357
  83.6 4.7 %collective-permute-start.18 = (bf16[768,512]{1,0:T(8,128)(2,1)S(1)}, bf16[768,512]{1,0:T(8,128)(2,1)S(1)}, u32[]{:S(2)}, u32[]{:S(2)}) collective-permute-start(bf16[768,512]{1,0:T(8,128)(2,1)S(1)} %get-tuple-element.71), channel_id=1, source_target_pairs={{2,1},{3,2},{6,5},{7,6},{10,9},{11,10},{14,13},{15,14},{18,17},{19... | collective-permute-start | bytes 2359304 | tf_op jit(solution)/shard_map/ppermute | solution.py:455
  88.3 3.6 %collective-permute-done.15.refs_14_ = bf16[768,512]{1,0:T(8,128)(2,1)S(1)} collective-permute-done((bf16[768,512]{1,0:T(8,128)(2,1)S(1)}, bf16[768,512]{1,0:T(8,128)(2,1)S(1)}, u32[]{:S(2)}, u32[]{:S(2)}) %collective-permute-start.15) | collective-permute-done | bytes 786464 | tf_op jit(solution)/shard_map/ppermute | solution.py:455
  92.0 3.3 %shard_map.89 = (bf16[768,512]{1,0:T(8,128)(2,1)S(1)}, bf16[768,512]{1,0:T(8,128)(2,1)S(1)}) custom-call(s32[3]{0:T(128)S(1)} %copy-done.10, bf16[384,512]{1,0:T(8,128)(2,1)S(1)} %copy-done.5, bf16[384,512]{1,0:T(8,128)(2,1)S(1)} %collective-permute-done.7.refs_2_, bf16[384,512]{1,0:T(8,128)(2,1)} %collective-permute-done.8.refs_3_, ...), custom_call_target="tpu_custom_call" | custom-call | flops 2280000000 | tf_op jit(solution)/shard_map/pallas_call | solution.py:357
  96.6 4.6 %collective-permute-start.20 = (bf16[768,512]{1,0:T(8,128)(2,1)S(1)}, bf16[768,512]{1,0:T(8,128)(2,1)S(1)}, u32[]{:S(2)}, u32[]{:S(2)}) collective-permute-start(bf16[768,512]{1,0:T(8,128)(2,1)S(1)} %get-tuple-element.74), channel_id=1, source_target_pairs={{2,1},{3,2},{6,5},{7,6},{10,9},{11,10},{14,13},{15,14},{18,17},{19... | collective-permute-start | bytes 2359304 | tf_op jit(solution)/shard_map/ppermute | solution.py:455
  101.9 1.6 collective-permute-done.17.refs_9_
  103.5 5.3 %collective-permute-done.18.refs_10_ = bf16[768,512]{1,0:T(8,128)(2,1)S(1)} collective-permute-done((bf16[768,512]{1,0:T(8,128)(2,1)S(1)}, bf16[768,512]{1,0:T(8,128)(2,1)S(1)}, u32[]{:S(2)}, u32[]{:S(2)}) %collective-permute-start.18) | collective-permute-done | bytes 786464 | tf_op jit(solution)/shard_map/ppermute | solution.py:455
  108.8 6.6 %shard_map.90 = (bf16[768,512]{1,0:T(8,128)(2,1)S(1)}, bf16[768,512]{1,0:T(8,128)(2,1)S(1)}) custom-call(s32[3]{0:T(128)S(1)} %copy-done.10, bf16[768,512]{1,0:T(8,128)(2,1)S(1)} %copy-done.4, bf16[768,512]{1,0:T(8,128)(2,1)} %collective-permute-done.1.refs_2_, bf16[768,512]{1,0:T(8,128)(2,1)} %collective-permute-done.2.refs_3_, ...), custom_call_target="tpu_custom_call" | custom-call | flops 2280000000 | tf_op jit(solution)/shard_map/pallas_call | solution.py:357
  115.4 2.1 %collective-permute-start.22 = (bf16[768,512]{1,0:T(8,128)(2,1)S(1)}, bf16[768,512]{1,0:T(8,128)(2,1)S(1)}, u32[]{:S(2)}, u32[]{:S(2)}) collective-permute-start(bf16[768,512]{1,0:T(8,128)(2,1)S(1)} %get-tuple-element.77), channel_id=1, source_target_pairs={{0,1},{1,2},{2,3},{4,5},{5,6},{6,7},{8,9},{9,10},{10,11},{12,13},{... | collective-permute-start | bytes 2359304 | tf_op jit(solution)/shard_map/ppermute | solution.py:454
  117.6 3.9 %collective-permute-start.23 = (bf16[768,512]{1,0:T(8,128)(2,1)S(1)}, bf16[768,512]{1,0:T(8,128)(2,1)S(1)}, u32[]{:S(2)}, u32[]{:S(2)}) collective-permute-start(bf16[768,512]{1,0:T(8,128)(2,1)S(1)} %get-tuple-element.78), channel_id=1, source_target_pairs={{1,0},{2,1},{3,2},{5,4},{6,5},{7,6},{9,8},{10,9},{11,10},{13,12},{... | collective-permute-start | bytes 2359304 | tf_op jit(solution)/shard_map/ppermute | solution.py:455
  121.5 4.2 %collective-permute-done.20.refs_14_ = bf16[768,512]{1,0:T(8,128)(2,1)S(1)} collective-permute-done((bf16[768,512]{1,0:T(8,128)(2,1)S(1)}, bf16[768,512]{1,0:T(8,128)(2,1)S(1)}, u32[]{:S(2)}, u32[]{:S(2)}) %collective-permute-start.20) | collective-permute-done | bytes 786464 | tf_op jit(solution)/shard_map/ppermute | solution.py:455
  125.7 5.6 %shard_map.91 = (bf16[768,512]{1,0:T(8,128)(2,1)S(1)}, bf16[768,512]{1,0:T(8,128)(2,1)S(1)}) custom-call(s32[3]{0:T(128)S(1)} %copy-done.10, bf16[384,512]{1,0:T(8,128)(2,1)S(1)} %copy-done.5, bf16[384,512]{1,0:T(8,128)(2,1)S(1)} %collective-permute-done.7.refs_2_, bf16[384,512]{1,0:T(8,128)(2,1)} %collective-permute-done.8.refs_3_, ...), custom_call_target="tpu_custom_call" | custom-call | flops 2280000000 | tf_op jit(solution)/shard_map/pallas_call | solution.py:357
  131.3 1.9 %collective-permute-start.24 = (bf16[768,512]{1,0:T(8,128)(2,1)S(1)}, bf16[768,512]{1,0:T(8,128)(2,1)S(1)}, u32[]{:S(2)}, u32[]{:S(2)}) collective-permute-start(bf16[768,512]{1,0:T(8,128)(2,1)S(1)} %get-tuple-element.80), channel_id=1, source_target_pairs={{0,1},{1,2},{2,3},{4,5},{5,6},{6,7},{8,9},{9,10},{10,11},{12,13},{... | collective-permute-start | bytes 2359304 | tf_op jit(solution)/shard_map/ppermute | solution.py:454
  133.2 4.1 %collective-permute-start.25 = (bf16[768,512]{1,0:T(8,128)(2,1)S(1)}, bf16[768,512]{1,0:T(8,128)(2,1)S(1)}, u32[]{:S(2)}, u32[]{:S(2)}) collective-permute-start(bf16[768,512]{1,0:T(8,128)(2,1)S(1)} %get-tuple-element.81), channel_id=1, source_target_pairs={{1,0},{2,1},{3,2},{5,4},{6,5},{7,6},{9,8},{10,9},{11,10},{13,12},{... | collective-permute-start | bytes 2359304 | tf_op jit(solution)/shard_map/ppermute | solution.py:455
  137.3 5.2 %collective-permute-done.23.refs_8_ = bf16[768,512]{1,0:T(8,128)(2,1)S(1)} collective-permute-done((bf16[768,512]{1,0:T(8,128)(2,1)S(1)}, bf16[768,512]{1,0:T(8,128)(2,1)S(1)}, u32[]{:S(2)}, u32[]{:S(2)}) %collective-permute-start.23) | collective-permute-done | bytes 786464 | tf_op jit(solution)/shard_map/ppermute | solution.py:455
  142.5 4.1 %shard_map.92.part = bf16[768,512]{1,0:T(8,128)(2,1)S(1)} custom-call(s32[3]{0:T(128)S(1)} %copy-done.10, bf16[768,512]{1,0:T(8,128)(2,1)S(1)} %copy-done.4, bf16[768,512]{1,0:T(8,128)(2,1)} %collective-permute-done.1.refs_2_, bf16[768,512]{1,0:T(8,128)(2,1)} %collective-permute-done.2.refs_3_, bf16[768,512]{1,0:T(8,128)(2,1)} %collective-permute-done.4.refs_4_, ...), custom_call_target="tpu_custom_call" | custom-call | flops 2280000000 | tf_op jit(solution)/shard_map/pallas_call | solution.py:357
  147.2 3.4 %shard_map.94.total = f32[768,512]{1,0:T(8,128)S(1)} custom-call(s32[3]{0:T(128)S(1)} %copy-done.10, bf16[384,512]{1,0:T(8,128)(2,1)S(1)} %copy-done.5, bf16[384,512]{1,0:T(8,128)(2,1)S(1)} %collective-permute-done.7.refs_2_, bf16[384,512]{1,0:T(8,128)(2,1)} %collective-permute-done.8.refs_3_, bf16[384,512]{1,0:T(8,128)(2,1)S(1)} %collective-permute-done.9.refs_4_, ...), custom_call_target="tpu_custom_call" | custom-call | flops 2280000000 | tf_op jit(solution)/shard_map/pallas_call | solution.py:357
  152.0 6.6 %collective-permute-done.25.from_right = bf16[768,512]{1,0:T(8,128)(2,1)S(1)} collective-permute-done((bf16[768,512]{1,0:T(8,128)(2,1)S(1)}, bf16[768,512]{1,0:T(8,128)(2,1)S(1)}, u32[]{:S(2)}, u32[]{:S(2)}) %collective-permute-start.25) | collective-permute-done | bytes 786464 | tf_op jit(solution)/shard_map/ppermute | solution.py:455
  158.6 2.6 %shard_map.95 = bf16[1536,512]{1,0:T(8,128)(2,1)} custom-call(bf16[384,384]{1,0:T(8,128)(2,1)S(1)} %copy-done.8, bf16[384,384]{1,0:T(8,128)(2,1)S(1)} %copy-done.7, bf16[1536,384]{1,0:T(8,128)(2,1)S(1)} %copy-done.6, f32[384,1]{1,0:T(8,128)S(1)} %copy-done.9, bf16[1152,512]{1,0:T(8,128)(2,1)S(1)} %shard_map.93.base, f32[768,512]{1,0:T(8,128)S(1)} %shard_map.94.total, ...), custom_call_target="tpu_custom_call" | custom-call | flops 2000000000 | tf_op jit(solution)/shard_map/pallas_call | solution.py:523
  (81 shorter events, 22.1 us)
Async XLA Ops:
  0.0 24.5 %copy-start = (s32[4,8192]{1,0:T(4,128)S(1)}, s32[4,8192]{1,0:T(4,128)}, u32[]{:S(2)}) copy-start(s32[4,8192]{1,0:T(4,128)} %param.13) | copy-start | bytes 393220
  0.9 4.1 %collective-permute-start = (bf16[1,48,512]{2,1,0:T(8,128)(2,1)S(1)}, bf16[1,48,512]{2,1,0:T(8,128)(2,1)S(1)}, u32[]{:S(2)}, u32[]{:S(2)}) collective-permute-start(bf16[1,48,512]{2,1,0:T(8,128)(2,1)S(1)} %slice_select_fusion), channel_id=1, source_target_pairs={{0,16},{16,0},{1,17},{17,1},{2,18},{18,2},{3,19},{19,3},{4,20},{20... | collective-permute-start | bytes 147464 | tf_op jit(solution)/shard_map/ppermute | solution.py:389
  12.7 25.1 %collective-permute-start.3 = (bf16[512,1024]{1,0:T(8,128)(2,1)}, bf16[512,1024]{1,0:T(8,128)(2,1)S(1)}, u32[]{:S(2)}, u32[]{:S(2)}) collective-permute-start(bf16[512,1024]{1,0:T(8,128)(2,1)} %get-tuple-element.57.refs_5_.refs_9_), channel_id=1, source_target_pairs={{0,16},{16,0},{1,17},{17,1},{2,18},{18,2},{3,19},{19,3},{4,20},{20... | collective-permute-start | bytes 3145736 | tf_op jit(solution)/shard_map/ppermute | solution.py:443
  14.3 23.5 %collective-permute-start.2 = (bf16[768,512]{1,0:T(8,128)(2,1)}, bf16[768,512]{1,0:T(8,128)(2,1)}, u32[]{:S(2)}, u32[]{:S(2)}) collective-permute-start(bf16[768,512]{1,0:T(8,128)(2,1)} %get-tuple-element.55.refs_1_), channel_id=1, source_target_pairs={{0,8},{4,12},{8,0},{12,4},{1,9},{5,13},{9,1},{13,5},{2,10},{6,14},... | collective-permute-start | bytes 2359304 | tf_op jit(solution)/shard_map/ppermute | solution.py:450
  18.3 20.0 %all-to-all-start = ((bf16[16,48,384]{2,1,0:T(8,128)(2,1)}), bf16[16,48,384]{2,1,0:T(8,128)(2,1)}, u32[]{:S(2)}, u32[]{:S(2)}) async-start(bf16[16,48,384]{2,1,0:T(8,128)(2,1)} %shard_map.84), calls=%async_computation | async-start | bytes 1179648 | tf_op jit(solution)/shard_map/all_to_all | solution.py:451
  25.1 13.2 %collective-permute-start.1 = (bf16[768,512]{1,0:T(8,128)(2,1)S(1)}, bf16[768,512]{1,0:T(8,128)(2,1)}, u32[]{:S(2)}, u32[]{:S(2)}) collective-permute-start(bf16[768,512]{1,0:T(8,128)(2,1)S(1)} %copy-done.4), channel_id=1, source_target_pairs={{0,4},{4,0},{8,12},{12,8},{1,5},{5,1},{9,13},{13,9},{2,6},{6,2},{1... | collective-permute-start | bytes 2359304 | tf_op jit(solution)/shard_map/ppermute | solution.py:465
  25.3 15.1 %copy-start.3 = (bf16[512,1024]{1,0:T(8,128)(2,1)S(1)}, bf16[512,1024]{1,0:T(8,128)(2,1)}, u32[]{:S(2)}) copy-start(bf16[512,1024]{1,0:T(8,128)(2,1)} %get-tuple-element.57.refs_5_.refs_9_) | copy-start | bytes 3145732
  25.3 15.1 %copy-start.10 = (s32[3]{0:T(128)S(1)}, s32[3]{0:T(128)}, u32[]{:S(2)}) copy-start(s32[3]{0:T(128)} %pad_add_fusion.refs_0_) | copy-start | bytes 40
  37.8 2.6 %collective-permute-start.4 = (bf16[768,512]{1,0:T(8,128)(2,1)}, bf16[768,512]{1,0:T(8,128)(2,1)}, u32[]{:S(2)}, u32[]{:S(2)}) collective-permute-start(bf16[768,512]{1,0:T(8,128)(2,1)} %collective-permute-done.2.refs_3_), channel_id=1, source_target_pairs={{0,4},{4,0},{8,12},{12,8},{1,5},{5,1},{9,13},{13,9},{2,6},{6,2},{1... | collective-permute-start | bytes 2359304 | tf_op jit(solution)/shard_map/ppermute | solution.py:466
  37.8 11.7 %collective-permute-start.8 = (bf16[384,512]{1,0:T(8,128)(2,1)S(1)}, bf16[384,512]{1,0:T(8,128)(2,1)}, u32[]{:S(2)}, u32[]{:S(2)}) collective-permute-start(bf16[384,512]{1,0:T(8,128)(2,1)S(1)} %copy-done.5), channel_id=1, source_target_pairs={{0,8},{4,12},{8,0},{12,4},{1,9},{5,13},{9,1},{13,5},{2,10},{6,14},... | collective-permute-start | bytes 1179656 | tf_op jit(solution)/shard_map/ppermute | solution.py:450
  42.1 20.5 %collective-permute-start.5 = (bf16[768,512]{1,0:T(8,128)(2,1)S(1)}, bf16[768,512]{1,0:T(8,128)(2,1)S(1)}, u32[]{:S(2)}, u32[]{:S(2)}) collective-permute-start(bf16[768,512]{1,0:T(8,128)(2,1)S(1)} %get-tuple-element.59), channel_id=1, source_target_pairs={{0,1},{4,5},{8,9},{12,13},{16,17},{20,21},{24,25},{28,29}} | collective-permute-start | bytes 2359304 | tf_op jit(solution)/shard_map/ppermute | solution.py:454
  42.8 23.2 %collective-permute-start.6 = (bf16[768,512]{1,0:T(8,128)(2,1)S(1)}, bf16[768,512]{1,0:T(8,128)(2,1)S(1)}, u32[]{:S(2)}, u32[]{:S(2)}) collective-permute-start(bf16[768,512]{1,0:T(8,128)(2,1)S(1)} %get-tuple-element.60), channel_id=1, source_target_pairs={{3,2},{7,6},{11,10},{15,14},{19,18},{23,22},{27,26},{31,30}} | collective-permute-start | bytes 2359304 | tf_op jit(solution)/shard_map/ppermute | solution.py:455
  51.8 10.8 %collective-permute-start.11 = (bf16[384,512]{1,0:T(8,128)(2,1)S(1)}, bf16[384,512]{1,0:T(8,128)(2,1)S(1)}, u32[]{:S(2)}, u32[]{:S(2)}) collective-permute-start(bf16[384,512]{1,0:T(8,128)(2,1)S(1)} %shard_map.86.refs_5_), channel_id=1, source_target_pairs={{0,8},{4,12},{8,0},{12,4},{1,9},{5,13},{9,1},{13,5},{2,10},{6,14},... | collective-permute-start | bytes 1179656 | tf_op jit(solution)/shard_map/ppermute | solution.py:499
  52.1 18.9 %copy-start.2 = (bf16[512,1024]{1,0:T(8,128)(2,1)S(1)}, bf16[512,1024]{1,0:T(8,128)(2,1)}, u32[]{:S(2)}) copy-start(bf16[512,1024]{1,0:T(8,128)(2,1)} %get-tuple-element.76.refs_7_.refs_11_) | copy-start | bytes 3145732
  52.1 26.1 %collective-permute-start.13 = (bf16[512,1024]{1,0:T(8,128)(2,1)S(1)}, bf16[512,1024]{1,0:T(8,128)(2,1)S(1)}, u32[]{:S(2)}, u32[]{:S(2)}) collective-permute-start(bf16[512,1024]{1,0:T(8,128)(2,1)S(1)} %copy-done.1), channel_id=1, source_target_pairs={{0,16},{16,0},{1,17},{17,1},{2,18},{18,2},{3,19},{19,3},{4,20},{20... | collective-permute-start | bytes 3145736 | tf_op jit(solution)/shard_map/ppermute | solution.py:443
  53.0 13.0 %collective-permute-start.7 = (bf16[384,512]{1,0:T(8,128)(2,1)S(1)}, bf16[384,512]{1,0:T(8,128)(2,1)S(1)}, u32[]{:S(2)}, u32[]{:S(2)}) collective-permute-start(bf16[384,512]{1,0:T(8,128)(2,1)S(1)} %copy-done.5), channel_id=1, source_target_pairs={{0,4},{4,0},{8,12},{12,8},{1,5},{5,1},{9,13},{13,9},{2,6},{6,2},{1... | collective-permute-start | bytes 1179656 | tf_op jit(solution)/shard_map/ppermute | solution.py:465
  62.5 3.5 %collective-permute-start.10 = (bf16[384,512]{1,0:T(8,128)(2,1)S(1)}, bf16[384,512]{1,0:T(8,128)(2,1)S(1)}, u32[]{:S(2)}, u32[]{:S(2)}) collective-permute-start(bf16[384,512]{1,0:T(8,128)(2,1)S(1)} %shard_map.86.refs_5_), channel_id=1, source_target_pairs={{0,4},{4,0},{8,12},{12,8},{1,5},{5,1},{9,13},{13,9},{2,6},{6,2},{1... | collective-permute-start | bytes 1179656 | tf_op jit(solution)/shard_map/ppermute | solution.py:465
  62.5 3.5 %collective-permute-start.9 = (bf16[384,512]{1,0:T(8,128)(2,1)}, bf16[384,512]{1,0:T(8,128)(2,1)S(1)}, u32[]{:S(2)}, u32[]{:S(2)}) collective-permute-start(bf16[384,512]{1,0:T(8,128)(2,1)} %collective-permute-done.8.refs_3_), channel_id=1, source_target_pairs={{0,4},{4,0},{8,12},{12,8},{1,5},{5,1},{9,13},{13,9},{2,6},{6,2},{1... | collective-permute-start | bytes 1179656 | tf_op jit(solution)/shard_map/ppermute | solution.py:466
  66.0 1.7 %collective-permute-start.12 = (bf16[384,512]{1,0:T(8,128)(2,1)S(1)}, bf16[384,512]{1,0:T(8,128)(2,1)S(1)}, u32[]{:S(2)}, u32[]{:S(2)}) collective-permute-start(bf16[384,512]{1,0:T(8,128)(2,1)S(1)} %collective-permute-done.11.refs_7_), channel_id=1, source_target_pairs={{0,4},{4,0},{8,12},{12,8},{1,5},{5,1},{9,13},{13,9},{2,6},{6,2},{1... | collective-permute-start | bytes 1179656 | tf_op jit(solution)/shard_map/ppermute | solution.py:466
  69.0 19.4 %collective-permute-start.14 = (bf16[768,512]{1,0:T(8,128)(2,1)S(1)}, bf16[768,512]{1,0:T(8,128)(2,1)S(1)}, u32[]{:S(2)}, u32[]{:S(2)}) collective-permute-start(bf16[768,512]{1,0:T(8,128)(2,1)S(1)} %get-tuple-element.66), channel_id=1, source_target_pairs={{0,1},{4,5},{8,9},{12,13},{16,17},{20,21},{24,25},{28,29}} | collective-permute-start | bytes 2359304 | tf_op jit(solution)/shard_map/ppermute | solution.py:454
  69.7 22.3 %collective-permute-start.15 = (bf16[768,512]{1,0:T(8,128)(2,1)S(1)}, bf16[768,512]{1,0:T(8,128)(2,1)S(1)}, u32[]{:S(2)}, u32[]{:S(2)}) collective-permute-start(bf16[768,512]{1,0:T(8,128)(2,1)S(1)} %get-tuple-element.67), channel_id=1, source_target_pairs={{3,2},{7,6},{11,10},{15,14},{19,18},{23,22},{27,26},{31,30}} | collective-permute-start | bytes 2359304 | tf_op jit(solution)/shard_map/ppermute | solution.py:455
  71.0 30.1 %collective-permute-start.16 = (bf16[512,1024]{1,0:T(8,128)(2,1)S(1)}, bf16[512,1024]{1,0:T(8,128)(2,1)S(1)}, u32[]{:S(2)}, u32[]{:S(2)}) collective-permute-start(bf16[512,1024]{1,0:T(8,128)(2,1)S(1)} %copy-done.2), channel_id=1, source_target_pairs={{0,16},{16,0},{1,17},{17,1},{2,18},{18,2},{3,19},{19,3},{4,20},{20... | collective-permute-start | bytes 3145736 | tf_op jit(solution)/shard_map/ppermute | solution.py:443
  82.3 21.2 %collective-permute-start.17 = (bf16[768,512]{1,0:T(8,128)(2,1)S(1)}, bf16[768,512]{1,0:T(8,128)(2,1)S(1)}, u32[]{:S(2)}, u32[]{:S(2)}) collective-permute-start(bf16[768,512]{1,0:T(8,128)(2,1)S(1)} %get-tuple-element.70), channel_id=1, source_target_pairs={{0,1},{1,2},{4,5},{5,6},{8,9},{9,10},{12,13},{13,14},{16,17},{17,1... | collective-permute-start | bytes 2359304 | tf_op jit(solution)/shard_map/ppermute | solution.py:454
  83.6 17.5 %copy-start.12 = (bf16[512,1024]{1,0:T(8,128)(2,1)S(1)}, bf16[512,1024]{1,0:T(8,128)(2,1)}, u32[]{:S(2)}) copy-start(bf16[512,1024]{1,0:T(8,128)(2,1)} %get-tuple-element.83.refs_5_.refs_9_) | copy-start | bytes 3145732
  83.6 25.2 %collective-permute-start.18 = (bf16[768,512]{1,0:T(8,128)(2,1)S(1)}, bf16[768,512]{1,0:T(8,128)(2,1)S(1)}, u32[]{:S(2)}, u32[]{:S(2)}) collective-permute-start(bf16[768,512]{1,0:T(8,128)(2,1)S(1)} %get-tuple-element.71), channel_id=1, source_target_pairs={{2,1},{3,2},{6,5},{7,6},{10,9},{11,10},{14,13},{15,14},{18,17},{19... | collective-permute-start | bytes 2359304 | tf_op jit(solution)/shard_map/ppermute | solution.py:455
  95.3 26.2 %collective-permute-start.19 = (bf16[768,512]{1,0:T(8,128)(2,1)S(1)}, bf16[768,512]{1,0:T(8,128)(2,1)S(1)}, u32[]{:S(2)}, u32[]{:S(2)}) collective-permute-start(bf16[768,512]{1,0:T(8,128)(2,1)S(1)} %get-tuple-element.73), channel_id=1, source_target_pairs={{0,1},{1,2},{4,5},{5,6},{8,9},{9,10},{12,13},{13,14},{16,17},{17,1... | collective-permute-start | bytes 2359304 | tf_op jit(solution)/shard_map/ppermute | solution.py:454
  96.6 29.1 %collective-permute-start.20 = (bf16[768,512]{1,0:T(8,128)(2,1)S(1)}, bf16[768,512]{1,0:T(8,128)(2,1)S(1)}, u32[]{:S(2)}, u32[]{:S(2)}) collective-permute-start(bf16[768,512]{1,0:T(8,128)(2,1)S(1)} %get-tuple-element.74), channel_id=1, source_target_pairs={{2,1},{3,2},{6,5},{7,6},{10,9},{11,10},{14,13},{15,14},{18,17},{19... | collective-permute-start | bytes 2359304 | tf_op jit(solution)/shard_map/ppermute | solution.py:455
  101.2 36.1 %collective-permute-start.21 = (bf16[512,1024]{1,0:T(8,128)(2,1)S(1)}, bf16[512,1024]{1,0:T(8,128)(2,1)S(1)}, u32[]{:S(2)}, u32[]{:S(2)}) collective-permute-start(bf16[512,1024]{1,0:T(8,128)(2,1)S(1)} %copy-done.12), channel_id=1, source_target_pairs={{0,16},{16,0},{1,17},{17,1},{2,18},{18,2},{3,19},{19,3},{4,20},{20... | collective-permute-start | bytes 3145736 | tf_op jit(solution)/shard_map/ppermute | solution.py:443
  115.4 21.9 %collective-permute-start.22 = (bf16[768,512]{1,0:T(8,128)(2,1)S(1)}, bf16[768,512]{1,0:T(8,128)(2,1)S(1)}, u32[]{:S(2)}, u32[]{:S(2)}) collective-permute-start(bf16[768,512]{1,0:T(8,128)(2,1)S(1)} %get-tuple-element.77), channel_id=1, source_target_pairs={{0,1},{1,2},{2,3},{4,5},{5,6},{6,7},{8,9},{9,10},{10,11},{12,13},{... | collective-permute-start | bytes 2359304 | tf_op jit(solution)/shard_map/ppermute | solution.py:454
  117.6 25.0 %collective-permute-start.23 = (bf16[768,512]{1,0:T(8,128)(2,1)S(1)}, bf16[768,512]{1,0:T(8,128)(2,1)S(1)}, u32[]{:S(2)}, u32[]{:S(2)}) collective-permute-start(bf16[768,512]{1,0:T(8,128)(2,1)S(1)} %get-tuple-element.78), channel_id=1, source_target_pairs={{1,0},{2,1},{3,2},{5,4},{6,5},{7,6},{9,8},{10,9},{11,10},{13,12},{... | collective-permute-start | bytes 2359304 | tf_op jit(solution)/shard_map/ppermute | solution.py:455
  131.3 20.7 %collective-permute-start.24 = (bf16[768,512]{1,0:T(8,128)(2,1)S(1)}, bf16[768,512]{1,0:T(8,128)(2,1)S(1)}, u32[]{:S(2)}, u32[]{:S(2)}) collective-permute-start(bf16[768,512]{1,0:T(8,128)(2,1)S(1)} %get-tuple-element.80), channel_id=1, source_target_pairs={{0,1},{1,2},{2,3},{4,5},{5,6},{6,7},{8,9},{9,10},{10,11},{12,13},{... | collective-permute-start | bytes 2359304 | tf_op jit(solution)/shard_map/ppermute | solution.py:454
  133.2 25.4 %collective-permute-start.25 = (bf16[768,512]{1,0:T(8,128)(2,1)S(1)}, bf16[768,512]{1,0:T(8,128)(2,1)S(1)}, u32[]{:S(2)}, u32[]{:S(2)}) collective-permute-start(bf16[768,512]{1,0:T(8,128)(2,1)S(1)} %get-tuple-element.81), channel_id=1, source_target_pairs={{1,0},{2,1},{3,2},{5,4},{6,5},{7,6},{9,8},{10,9},{11,10},{13,12},{... | collective-permute-start | bytes 2359304 | tf_op jit(solution)/shard_map/ppermute | solution.py:455
  (15 other events, 155.9 us)
where the time goes:
time: 162 us; the launch traced here: 161 us
  waiting for transfers between devices  64.9 us (40%)
  Pallas kernels  50.6 us (31%)
  starting transfers between devices  41.2 us (25%)
  local copies, waits for them, and re-layouts  2.56 us (2%)
    pallas_call x8, Pallas kernels, hop(): pl.pallas_call(functools.partial(hop_kernel, t, size, wide, slots, len(bl...  29.9 us
    ppermute x6, waiting for transfers between devices, send(): lax.ppermute(value[1], 'mcol', left[n_col - 1 - t:])  27.9 us
    ppermute x6, starting transfers between devices, send(): lax.ppermute(value[1], 'mcol', left[n_col - 1 - t:])  19.8 us
    ppermute x2, waiting for transfers between devices, on_device(): far.append(lax.ppermute(value, 'mrow', flip[1]))  13.2 us
    ppermute x1, waiting for transfers between devices, on_device(): far.append(lax.ppermute(mine[count], 'mrow', flip[1]))  9.51 us
    ppermute x6, starting transfers between devices, send(): lax.ppermute(value[0], 'mcol', right[:t])  8.07 us
    pallas_call x1, Pallas kernels, on_device(): pl.pallas_call(functools.partial(read_kernel, count, shards), out_shape=[...  7.12 us
    ppermute x4, waiting for transfers between devices, on_device(): held.append((part, lax.ppermute(part, 'space', swap)))  6.42 us
  transfers between devices with their start and end apart: 27, of which 16 were waited for; matrix products, arithmetic and copies ran while one was open for 2% of the time, Pallas kernels for 25%

commit v1 on v0

--- a/solution.py
+++ b/solution.py
@@ -127,7 +127,7 @@
             stores.append(pltpu.make_async_copy(stage.at[j], parts[j], out_sem.at[j]))
     for copy in fetches:
         copy.start()
-    moves(cells_lane[...], fill.shape[0], fill, spare, on_rim)
+    moves(cells_lane[...].reshape(1, -1), fill.shape[0], fill, spare, on_rim)
     width_x, width_y, modes = dev.shape
     speed = courant[...]
     reach = jnp.abs(speed)
@@ -428,7 +428,7 @@
         ][: shards * 3],
         compiler_params=params,
         cost_estimate=takes(6),
-    )(where, deviation, courant, lane_cells, *edges, *([] if wide else [order, collide]))
+    )(where, deviation, courant, hole_cells, *edges, *([] if wide else [order, collide]))
     read = mine.pop()
     payload = pl.pallas_call(
         functools.partial(payload_kernel, n_row, n_col),

time: 162 us -> 162 us (level)
    ppermute x6, waiting for transfers between devices: 27.9 us -> 31.5 us  [send(): lax.ppermute(value[1], 'mcol', left[n_col - 1 - t:])]
    ppermute x2, waiting for transfers between devices: 13.2 us -> 11.1 us  [on_device(): far.append(lax.ppermute(value, 'mrow', flip[1]))]
  transfers between devices with their start and end apart: 27 -> 27, of which waited for: 16 -> 16; matrix products, arithmetic and copies ran while one was open for 2% -> 1% of each run, Pallas kernels for 25% -> 25%
where the time goes in v1:
time: 162 us; the launch traced here: 161 us
  waiting for transfers between devices  64.4 us (40%)
  Pallas kernels  50.9 us (31%)
  starting transfers between devices  42.1 us (26%)
  local copies, waits for them, and re-layouts  1.89 us (1%)
    ppermute x6, waiting for transfers between devices, send(): lax.ppermute(value[1], 'mcol', left[n_col - 1 - t:])  31.5 us
    pallas_call x8, Pallas kernels, hop(): pl.pallas_call(functools.partial(hop_kernel, t, size, wide, slots, len(bl...  30.1 us
    ppermute x6, starting transfers between devices, send(): lax.ppermute(value[1], 'mcol', left[n_col - 1 - t:])  19.8 us
    ppermute x2, waiting for transfers between devices, on_device(): far.append(lax.ppermute(value, 'mrow', flip[1]))  11.1 us
    ppermute x1, waiting for transfers between devices, on_device(): far.append(lax.ppermute(mine[count], 'mrow', flip[1]))  8.72 us
    ppermute x6, starting transfers between devices, send(): lax.ppermute(value[0], 'mcol', right[:t])  8.07 us
    pallas_call x1, Pallas kernels, on_device(): pl.pallas_call(functools.partial(read_kernel, count, shards), out_shape=[...  7.13 us
    all_to_all x1, starting transfers between devices, on_device(): lax.all_to_all(payload, ('mrow', 'mcol'), split_axis=0, concat_axis=0, ti...  6.19 us
  transfers between devices with their start and end apart: 27, of which 16 were waited for; matrix products, arithmetic and copies ran while one was open for 1% of the time, Pallas kernels for 25%

profile of v1, /device:TPU:20, one launch (start us, length us, event | category | flops | bytes accessed | tf_op | source)
XLA Modules:
  0.0 161.2 jit_solution(3714532569920718120)
XLA Ops:
  3.0 1.9 %collective-permute-done.refs_4_ = bf16[1,48,512]{2,1,0:T(8,128)(2,1)S(1)} collective-permute-done((bf16[1,48,512]{2,1,0:T(8,128)(2,1)S(1)}, bf16[1,48,512]{2,1,0:T(8,128)(2,1)S(1)}, u32[]{:S(2)}, u32[]{:S(2)}) %collective-permute-start) | collective-permute-done | bytes 49184 | tf_op jit(solution)/shard_map/ppermute | solution.py:389
  5.6 7.1 %shard_map.82 = (bf16[384,512]{1,0:T(8,128)(2,1)}, bf16[768,512]{1,0:T(8,128)(2,1)}, bf16[384,512]{1,0:T(8,128)(2,1)}, bf16[512,1024]{1,0:T(8,128)(2,1)}, bf16[5...) custom-call(s32[3]{0:T(128)} %pad_add_fusion.refs_0_, ...), custom_call_target="tpu_custom_call" | custom-call | flops 3000000000 | tf_op jit(solution)/shard_map/pallas_call | solution.py:411
  12.7 1.6 collective-permute-start.3
  15.4 3.6 %shard_map.84 = bf16[16,48,384]{2,1,0:T(8,128)(2,1)} custom-call(s32[1,384]{1,0:T(1,128)} %broadcast_in_dim.6.cells_lane, bf16[1536,512]{1,0:T(8,128)(2,1)} %get-tuple-element.53.read), custom_call_target="tpu_custom_call" | custom-call | flops 1500000000 | tf_op jit(solution)/shard_map/pallas_call | solution.py:433
  18.9 6.2 %all-to-all-start = ((bf16[16,48,384]{2,1,0:T(8,128)(2,1)}), bf16[16,48,384]{2,1,0:T(8,128)(2,1)}, u32[]{:S(2)}, u32[]{:S(2)}) async-start(bf16[16,48,384]{2,1,0:T(8,128)(2,1)} %shard_map.84), calls=%async_computation | async-start | bytes 1179648 | tf_op jit(solution)/shard_map/all_to_all | solution.py:451
  25.9 4.6 %shard_map.83 = (bf16[4,512,512]{2,1,0:T(8,128)(2,1)}, bf16[1536,384]{1,0:T(8,128)(2,1)}, bf16[384,384]{1,0:T(8,128)(2,1)}, bf16[768,384]{1,0:T(8,128)(2,1)}, bf...) custom-call(s32[1,384]{1,0:T(1,128)} %broadcast_in_dim.6.cells_lane, ...), custom_call_target="tpu_custom_call" | custom-call | flops 2000000000 | tf_op jit(solution)/shard_map/pallas_call | solution.py:470
  30.5 6.0 %collective-permute-done.2.refs_3_ = bf16[768,512]{1,0:T(8,128)(2,1)} collective-permute-done((bf16[768,512]{1,0:T(8,128)(2,1)}, bf16[768,512]{1,0:T(8,128)(2,1)}, u32[]{:S(2)}, u32[]{:S(2)}) %collective-permute-start.2) | collective-permute-done | bytes 786464 | tf_op jit(solution)/shard_map/ppermute | solution.py:450
  39.4 1.9 %shard_map.85 = (bf16[768,512]{1,0:T(8,128)(2,1)S(1)}, bf16[768,512]{1,0:T(8,128)(2,1)S(1)}) custom-call(s32[3]{0:T(128)S(1)} %copy-done.10, bf16[768,512]{1,0:T(8,128)(2,1)S(1)} %copy-done.4, bf16[768,512]{1,0:T(8,128)(2,1)} %collective-permute-done.1.refs_2_, bf16[768,512]{1,0:T(8,128)(2,1)} %collective-permute-done.2.refs_3_, ...), custom_call_target="tpu_custom_call" | custom-call | flops 2280000000 | tf_op jit(solution)/shard_map/pallas_call | solution.py:357
  43.3 5.1 %collective-permute-done.8.refs_3_ = bf16[384,512]{1,0:T(8,128)(2,1)} collective-permute-done((bf16[384,512]{1,0:T(8,128)(2,1)S(1)}, bf16[384,512]{1,0:T(8,128)(2,1)}, u32[]{:S(2)}, u32[]{:S(2)}) %collective-permute-start.8) | collective-permute-done | bytes 393248 | tf_op jit(solution)/shard_map/ppermute | solution.py:450
  48.5 2.2 %shard_map.86.refs_5_ = bf16[384,512]{1,0:T(8,128)(2,1)S(1)} custom-call(f32[4]{0:T(128)S(1)} %copy-done.13, bf16[16,48,384]{2,1,0:T(8,128)(2,1)} %all-to-all-done.arrived, bf16[4,512,512]{2,1,0:T(8,128)(2,1)S(1)} %copy-done.16, s32[1,384]{1,0:T(1,128)S(1)} %broadcast_in_dim.7.wall, s32[1,384]{1,0:T(1,128)S(1)} %copy-done.11, bf16[384,512]{1,0:T(8,128)(2,1)S(1)} %copy-done.17), custom_call_target="tpu_custom_call" | custom-call | flops 2000000000 | tf_op jit(solution)/shard_map/pallas_call | solution.py:490
  52.8 8.7 %collective-permute-done.11.refs_7_ = bf16[384,512]{1,0:T(8,128)(2,1)S(1)} collective-permute-done((bf16[384,512]{1,0:T(8,128)(2,1)S(1)}, bf16[384,512]{1,0:T(8,128)(2,1)S(1)}, u32[]{:S(2)}, u32[]{:S(2)}) %collective-permute-start.11) | collective-permute-done | bytes 393248 | tf_op jit(solution)/shard_map/ppermute | solution.py:499
  62.0 4.0 %collective-permute-done.6.refs_10_ = bf16[768,512]{1,0:T(8,128)(2,1)S(1)} collective-permute-done((bf16[768,512]{1,0:T(8,128)(2,1)S(1)}, bf16[768,512]{1,0:T(8,128)(2,1)S(1)}, u32[]{:S(2)}, u32[]{:S(2)}) %collective-permute-start.6) | collective-permute-done | bytes 786464 | tf_op jit(solution)/shard_map/ppermute | solution.py:455
  66.0 1.7 %collective-permute-done.12.refs_8_ = bf16[384,512]{1,0:T(8,128)(2,1)S(1)} collective-permute-done((bf16[384,512]{1,0:T(8,128)(2,1)S(1)}, bf16[384,512]{1,0:T(8,128)(2,1)S(1)}, u32[]{:S(2)}, u32[]{:S(2)}) %collective-permute-start.12) | collective-permute-done | bytes 393248 | tf_op jit(solution)/shard_map/ppermute | solution.py:466
  71.6 5.8 %collective-permute-done.13.refs_8_.refs_12_.refs_6_.refs_10_ = bf16[512,1024]{1,0:T(8,128)(2,1)S(1)} collective-permute-done((bf16[512,1024]{1,0:T(8,128)(2,1)S(1)}, bf16[512,1024]{1,0:T(8,128)(2,1)S(1)}, u32[]{:S(2)}, u32[]{:S(2)}) %collective-permute-start.13) | collective-permute-done | bytes 1048608 | tf_op jit(solution)/shard_map/ppermute | solution.py:443
  77.4 4.1 %shard_map.88 = (bf16[768,512]{1,0:T(8,128)(2,1)S(1)}, bf16[768,512]{1,0:T(8,128)(2,1)S(1)}) custom-call(s32[3]{0:T(128)S(1)} %copy-done.10, bf16[768,512]{1,0:T(8,128)(2,1)S(1)} %copy-done.4, bf16[768,512]{1,0:T(8,128)(2,1)} %collective-permute-done.1.refs_2_, bf16[768,512]{1,0:T(8,128)(2,1)} %collective-permute-done.2.refs_3_, ...), custom_call_target="tpu_custom_call" | custom-call | flops 2280000000 | tf_op jit(solution)/shard_map/pallas_call | solution.py:357
  82.8 4.7 %collective-permute-start.18 = (bf16[768,512]{1,0:T(8,128)(2,1)S(1)}, bf16[768,512]{1,0:T(8,128)(2,1)S(1)}, u32[]{:S(2)}, u32[]{:S(2)}) collective-permute-start(bf16[768,512]{1,0:T(8,128)(2,1)S(1)} %get-tuple-element.71), channel_id=1, source_target_pairs={{2,1},{3,2},{6,5},{7,6},{10,9},{11,10},{14,13},{15,14},{18,17},{19... | collective-permute-start | bytes 2359304 | tf_op jit(solution)/shard_map/ppermute | solution.py:455
  87.5 4.5 %collective-permute-done.15.refs_14_ = bf16[768,512]{1,0:T(8,128)(2,1)S(1)} collective-permute-done((bf16[768,512]{1,0:T(8,128)(2,1)S(1)}, bf16[768,512]{1,0:T(8,128)(2,1)S(1)}, u32[]{:S(2)}, u32[]{:S(2)}) %collective-permute-start.15) | collective-permute-done | bytes 786464 | tf_op jit(solution)/shard_map/ppermute | solution.py:455
  92.0 3.3 %shard_map.89 = (bf16[768,512]{1,0:T(8,128)(2,1)S(1)}, bf16[768,512]{1,0:T(8,128)(2,1)S(1)}) custom-call(s32[3]{0:T(128)S(1)} %copy-done.10, bf16[384,512]{1,0:T(8,128)(2,1)S(1)} %copy-done.5, bf16[384,512]{1,0:T(8,128)(2,1)S(1)} %collective-permute-done.7.refs_2_, bf16[384,512]{1,0:T(8,128)(2,1)} %collective-permute-done.8.refs_3_, ...), custom_call_target="tpu_custom_call" | custom-call | flops 2280000000 | tf_op jit(solution)/shard_map/pallas_call | solution.py:357
  96.6 4.6 %collective-permute-start.20 = (bf16[768,512]{1,0:T(8,128)(2,1)S(1)}, bf16[768,512]{1,0:T(8,128)(2,1)S(1)}, u32[]{:S(2)}, u32[]{:S(2)}) collective-permute-start(bf16[768,512]{1,0:T(8,128)(2,1)S(1)} %get-tuple-element.74), channel_id=1, source_target_pairs={{2,1},{3,2},{6,5},{7,6},{10,9},{11,10},{14,13},{15,14},{18,17},{19... | collective-permute-start | bytes 2359304 | tf_op jit(solution)/shard_map/ppermute | solution.py:455
  101.8 7.1 %collective-permute-done.18.refs_10_ = bf16[768,512]{1,0:T(8,128)(2,1)S(1)} collective-permute-done((bf16[768,512]{1,0:T(8,128)(2,1)S(1)}, bf16[768,512]{1,0:T(8,128)(2,1)S(1)}, u32[]{:S(2)}, u32[]{:S(2)}) %collective-permute-start.18) | collective-permute-done | bytes 786464 | tf_op jit(solution)/shard_map/ppermute | solution.py:455
  108.8 6.6 %shard_map.90 = (bf16[768,512]{1,0:T(8,128)(2,1)S(1)}, bf16[768,512]{1,0:T(8,128)(2,1)S(1)}) custom-call(s32[3]{0:T(128)S(1)} %copy-done.10, bf16[768,512]{1,0:T(8,128)(2,1)S(1)} %copy-done.4, bf16[768,512]{1,0:T(8,128)(2,1)} %collective-permute-done.1.refs_2_, bf16[768,512]{1,0:T(8,128)(2,1)} %collective-permute-done.2.refs_3_, ...), custom_call_target="tpu_custom_call" | custom-call | flops 2280000000 | tf_op jit(solution)/shard_map/pallas_call | solution.py:357
  115.4 2.1 %collective-permute-start.22 = (bf16[768,512]{1,0:T(8,128)(2,1)S(1)}, bf16[768,512]{1,0:T(8,128)(2,1)S(1)}, u32[]{:S(2)}, u32[]{:S(2)}) collective-permute-start(bf16[768,512]{1,0:T(8,128)(2,1)S(1)} %get-tuple-element.77), channel_id=1, source_target_pairs={{0,1},{1,2},{2,3},{4,5},{5,6},{6,7},{8,9},{9,10},{10,11},{12,13},{... | collective-permute-start | bytes 2359304 | tf_op jit(solution)/shard_map/ppermute | solution.py:454
  117.6 3.9 %collective-permute-start.23 = (bf16[768,512]{1,0:T(8,128)(2,1)S(1)}, bf16[768,512]{1,0:T(8,128)(2,1)S(1)}, u32[]{:S(2)}, u32[]{:S(2)}) collective-permute-start(bf16[768,512]{1,0:T(8,128)(2,1)S(1)} %get-tuple-element.78), channel_id=1, source_target_pairs={{1,0},{2,1},{3,2},{5,4},{6,5},{7,6},{9,8},{10,9},{11,10},{13,12},{... | collective-permute-start | bytes 2359304 | tf_op jit(solution)/shard_map/ppermute | solution.py:455
  121.5 4.2 %collective-permute-done.20.refs_14_ = bf16[768,512]{1,0:T(8,128)(2,1)S(1)} collective-permute-done((bf16[768,512]{1,0:T(8,128)(2,1)S(1)}, bf16[768,512]{1,0:T(8,128)(2,1)S(1)}, u32[]{:S(2)}, u32[]{:S(2)}) %collective-permute-start.20) | collective-permute-done | bytes 786464 | tf_op jit(solution)/shard_map/ppermute | solution.py:455
  125.7 5.6 %shard_map.91 = (bf16[768,512]{1,0:T(8,128)(2,1)S(1)}, bf16[768,512]{1,0:T(8,128)(2,1)S(1)}) custom-call(s32[3]{0:T(128)S(1)} %copy-done.10, bf16[384,512]{1,0:T(8,128)(2,1)S(1)} %copy-done.5, bf16[384,512]{1,0:T(8,128)(2,1)S(1)} %collective-permute-done.7.refs_2_, bf16[384,512]{1,0:T(8,128)(2,1)} %collective-permute-done.8.refs_3_, ...), custom_call_target="tpu_custom_call" | custom-call | flops 2280000000 | tf_op jit(solution)/shard_map/pallas_call | solution.py:357
  131.3 1.9 %collective-permute-start.24 = (bf16[768,512]{1,0:T(8,128)(2,1)S(1)}, bf16[768,512]{1,0:T(8,128)(2,1)S(1)}, u32[]{:S(2)}, u32[]{:S(2)}) collective-permute-start(bf16[768,512]{1,0:T(8,128)(2,1)S(1)} %get-tuple-element.80), channel_id=1, source_target_pairs={{0,1},{1,2},{2,3},{4,5},{5,6},{6,7},{8,9},{9,10},{10,11},{12,13},{... | collective-permute-start | bytes 2359304 | tf_op jit(solution)/shard_map/ppermute | solution.py:454
  133.2 4.1 %collective-permute-start.25 = (bf16[768,512]{1,0:T(8,128)(2,1)S(1)}, bf16[768,512]{1,0:T(8,128)(2,1)S(1)}, u32[]{:S(2)}, u32[]{:S(2)}) collective-permute-start(bf16[768,512]{1,0:T(8,128)(2,1)S(1)} %get-tuple-element.81), channel_id=1, source_target_pairs={{1,0},{2,1},{3,2},{5,4},{6,5},{7,6},{9,8},{10,9},{11,10},{13,12},{... | collective-permute-start | bytes 2359304 | tf_op jit(solution)/shard_map/ppermute | solution.py:455
  137.3 5.2 %collective-permute-done.23.refs_8_ = bf16[768,512]{1,0:T(8,128)(2,1)S(1)} collective-permute-done((bf16[768,512]{1,0:T(8,128)(2,1)S(1)}, bf16[768,512]{1,0:T(8,128)(2,1)S(1)}, u32[]{:S(2)}, u32[]{:S(2)}) %collective-permute-start.23) | collective-permute-done | bytes 786464 | tf_op jit(solution)/shard_map/ppermute | solution.py:455
  142.5 4.1 %shard_map.92.part = bf16[768,512]{1,0:T(8,128)(2,1)S(1)} custom-call(s32[3]{0:T(128)S(1)} %copy-done.10, bf16[768,512]{1,0:T(8,128)(2,1)S(1)} %copy-done.4, bf16[768,512]{1,0:T(8,128)(2,1)} %collective-permute-done.1.refs_2_, bf16[768,512]{1,0:T(8,128)(2,1)} %collective-permute-done.2.refs_3_, bf16[768,512]{1,0:T(8,128)(2,1)} %collective-permute-done.4.refs_4_, ...), custom_call_target="tpu_custom_call" | custom-call | flops 2280000000 | tf_op jit(solution)/shard_map/pallas_call | solution.py:357
  147.2 3.4 %shard_map.94.total = f32[768,512]{1,0:T(8,128)S(1)} custom-call(s32[3]{0:T(128)S(1)} %copy-done.10, bf16[384,512]{1,0:T(8,128)(2,1)S(1)} %copy-done.5, bf16[384,512]{1,0:T(8,128)(2,1)S(1)} %collective-permute-done.7.refs_2_, bf16[384,512]{1,0:T(8,128)(2,1)} %collective-permute-done.8.refs_3_, bf16[384,512]{1,0:T(8,128)(2,1)S(1)} %collective-permute-done.9.refs_4_, ...), custom_call_target="tpu_custom_call" | custom-call | flops 2280000000 | tf_op jit(solution)/shard_map/pallas_call | solution.py:357
  152.0 6.6 %collective-permute-done.25.from_right = bf16[768,512]{1,0:T(8,128)(2,1)S(1)} collective-permute-done((bf16[768,512]{1,0:T(8,128)(2,1)S(1)}, bf16[768,512]{1,0:T(8,128)(2,1)S(1)}, u32[]{:S(2)}, u32[]{:S(2)}) %collective-permute-start.25) | collective-permute-done | bytes 786464 | tf_op jit(solution)/shard_map/ppermute | solution.py:455
  158.6 2.6 %shard_map.95 = bf16[1536,512]{1,0:T(8,128)(2,1)} custom-call(bf16[384,384]{1,0:T(8,128)(2,1)S(1)} %copy-done.8, bf16[384,384]{1,0:T(8,128)(2,1)S(1)} %copy-done.7, bf16[1536,384]{1,0:T(8,128)(2,1)S(1)} %copy-done.6, f32[384,1]{1,0:T(8,128)S(1)} %copy-done.9, bf16[1152,512]{1,0:T(8,128)(2,1)S(1)} %shard_map.93.base, f32[768,512]{1,0:T(8,128)S(1)} %shard_map.94.total, ...), custom_call_target="tpu_custom_call" | custom-call | flops 2000000000 | tf_op jit(solution)/shard_map/pallas_call | solution.py:523
  (83 shorter events, 21.9 us)
Async XLA Ops:
  0.0 25.1 %copy-start = (s32[4,8192]{1,0:T(4,128)S(1)}, s32[4,8192]{1,0:T(4,128)}, u32[]{:S(2)}) copy-start(s32[4,8192]{1,0:T(4,128)} %param.13) | copy-start | bytes 393220
  0.9 4.1 %collective-permute-start = (bf16[1,48,512]{2,1,0:T(8,128)(2,1)S(1)}, bf16[1,48,512]{2,1,0:T(8,128)(2,1)S(1)}, u32[]{:S(2)}, u32[]{:S(2)}) collective-permute-start(bf16[1,48,512]{2,1,0:T(8,128)(2,1)S(1)} %slice_select_fusion), channel_id=1, source_target_pairs={{0,16},{16,0},{1,17},{17,1},{2,18},{18,2},{3,19},{19,3},{4,20},{20... | collective-permute-start | bytes 147464 | tf_op jit(solution)/shard_map/ppermute | solution.py:389
  12.7 24.0 %collective-permute-start.3 = (bf16[512,1024]{1,0:T(8,128)(2,1)}, bf16[512,1024]{1,0:T(8,128)(2,1)S(1)}, u32[]{:S(2)}, u32[]{:S(2)}) collective-permute-start(bf16[512,1024]{1,0:T(8,128)(2,1)} %get-tuple-element.57.refs_5_.refs_9_), channel_id=1, source_target_pairs={{0,16},{16,0},{1,17},{17,1},{2,18},{18,2},{3,19},{19,3},{4,20},{20... | collective-permute-start | bytes 3145736 | tf_op jit(solution)/shard_map/ppermute | solution.py:443
  14.3 22.2 %collective-permute-start.2 = (bf16[768,512]{1,0:T(8,128)(2,1)}, bf16[768,512]{1,0:T(8,128)(2,1)}, u32[]{:S(2)}, u32[]{:S(2)}) collective-permute-start(bf16[768,512]{1,0:T(8,128)(2,1)} %get-tuple-element.55.refs_1_), channel_id=1, source_target_pairs={{0,8},{4,12},{8,0},{12,4},{1,9},{5,13},{9,1},{13,5},{2,10},{6,14},... | collective-permute-start | bytes 2359304 | tf_op jit(solution)/shard_map/ppermute | solution.py:450
  18.9 19.9 %all-to-all-start = ((bf16[16,48,384]{2,1,0:T(8,128)(2,1)}), bf16[16,48,384]{2,1,0:T(8,128)(2,1)}, u32[]{:S(2)}, u32[]{:S(2)}) async-start(bf16[16,48,384]{2,1,0:T(8,128)(2,1)} %shard_map.84), calls=%async_computation | async-start | bytes 1179648 | tf_op jit(solution)/shard_map/all_to_all | solution.py:451
  25.7 13.1 %collective-permute-start.1 = (bf16[768,512]{1,0:T(8,128)(2,1)S(1)}, bf16[768,512]{1,0:T(8,128)(2,1)}, u32[]{:S(2)}, u32[]{:S(2)}) collective-permute-start(bf16[768,512]{1,0:T(8,128)(2,1)S(1)} %copy-done.4), channel_id=1, source_target_pairs={{0,4},{4,0},{8,12},{12,8},{1,5},{5,1},{9,13},{13,9},{2,6},{6,2},{1... | collective-permute-start | bytes 2359304 | tf_op jit(solution)/shard_map/ppermute | solution.py:465
  25.9 13.5 %copy-start.3 = (bf16[512,1024]{1,0:T(8,128)(2,1)S(1)}, bf16[512,1024]{1,0:T(8,128)(2,1)}, u32[]{:S(2)}) copy-start(bf16[512,1024]{1,0:T(8,128)(2,1)} %get-tuple-element.57.refs_5_.refs_9_) | copy-start | bytes 3145732
  25.9 13.5 %copy-start.10 = (s32[3]{0:T(128)S(1)}, s32[3]{0:T(128)}, u32[]{:S(2)}) copy-start(s32[3]{0:T(128)} %pad_add_fusion.refs_0_) | copy-start | bytes 40
  36.7 2.6 %collective-permute-start.4 = (bf16[768,512]{1,0:T(8,128)(2,1)}, bf16[768,512]{1,0:T(8,128)(2,1)}, u32[]{:S(2)}, u32[]{:S(2)}) collective-permute-start(bf16[768,512]{1,0:T(8,128)(2,1)} %collective-permute-done.2.refs_3_), channel_id=1, source_target_pairs={{0,4},{4,0},{8,12},{12,8},{1,5},{5,1},{9,13},{13,9},{2,6},{6,2},{1... | collective-permute-start | bytes 2359304 | tf_op jit(solution)/shard_map/ppermute | solution.py:466
  36.8 11.7 %collective-permute-start.8 = (bf16[384,512]{1,0:T(8,128)(2,1)S(1)}, bf16[384,512]{1,0:T(8,128)(2,1)}, u32[]{:S(2)}, u32[]{:S(2)}) collective-permute-start(bf16[384,512]{1,0:T(8,128)(2,1)S(1)} %copy-done.5), channel_id=1, source_target_pairs={{0,8},{4,12},{8,0},{12,4},{1,9},{5,13},{9,1},{13,5},{2,10},{6,14},... | collective-permute-start | bytes 1179656 | tf_op jit(solution)/shard_map/ppermute | solution.py:450
  41.3 20.3 %collective-permute-start.5 = (bf16[768,512]{1,0:T(8,128)(2,1)S(1)}, bf16[768,512]{1,0:T(8,128)(2,1)S(1)}, u32[]{:S(2)}, u32[]{:S(2)}) collective-permute-start(bf16[768,512]{1,0:T(8,128)(2,1)S(1)} %get-tuple-element.59), channel_id=1, source_target_pairs={{0,1},{4,5},{8,9},{12,13},{16,17},{20,21},{24,25},{28,29}} | collective-permute-start | bytes 2359304 | tf_op jit(solution)/shard_map/ppermute | solution.py:454
  42.0 24.0 %collective-permute-start.6 = (bf16[768,512]{1,0:T(8,128)(2,1)S(1)}, bf16[768,512]{1,0:T(8,128)(2,1)S(1)}, u32[]{:S(2)}, u32[]{:S(2)}) collective-permute-start(bf16[768,512]{1,0:T(8,128)(2,1)S(1)} %get-tuple-element.60), channel_id=1, source_target_pairs={{3,2},{7,6},{11,10},{15,14},{19,18},{23,22},{27,26},{31,30}} | collective-permute-start | bytes 2359304 | tf_op jit(solution)/shard_map/ppermute | solution.py:455
  50.7 10.8 %collective-permute-start.11 = (bf16[384,512]{1,0:T(8,128)(2,1)S(1)}, bf16[384,512]{1,0:T(8,128)(2,1)S(1)}, u32[]{:S(2)}, u32[]{:S(2)}) collective-permute-start(bf16[384,512]{1,0:T(8,128)(2,1)S(1)} %shard_map.86.refs_5_), channel_id=1, source_target_pairs={{0,8},{4,12},{8,0},{12,4},{1,9},{5,13},{9,1},{13,5},{2,10},{6,14},... | collective-permute-start | bytes 1179656 | tf_op jit(solution)/shard_map/ppermute | solution.py:499
  51.3 19.7 %copy-start.2 = (bf16[512,1024]{1,0:T(8,128)(2,1)S(1)}, bf16[512,1024]{1,0:T(8,128)(2,1)}, u32[]{:S(2)}) copy-start(bf16[512,1024]{1,0:T(8,128)(2,1)} %get-tuple-element.76.refs_7_.refs_11_) | copy-start | bytes 3145732
  51.3 26.1 %collective-permute-start.13 = (bf16[512,1024]{1,0:T(8,128)(2,1)S(1)}, bf16[512,1024]{1,0:T(8,128)(2,1)S(1)}, u32[]{:S(2)}, u32[]{:S(2)}) collective-permute-start(bf16[512,1024]{1,0:T(8,128)(2,1)S(1)} %copy-done.1), channel_id=1, source_target_pairs={{0,16},{16,0},{1,17},{17,1},{2,18},{18,2},{3,19},{19,3},{4,20},{20... | collective-permute-start | bytes 3145736 | tf_op jit(solution)/shard_map/ppermute | solution.py:443
  52.8 13.2 %collective-permute-start.7 = (bf16[384,512]{1,0:T(8,128)(2,1)S(1)}, bf16[384,512]{1,0:T(8,128)(2,1)S(1)}, u32[]{:S(2)}, u32[]{:S(2)}) collective-permute-start(bf16[384,512]{1,0:T(8,128)(2,1)S(1)} %copy-done.5), channel_id=1, source_target_pairs={{0,4},{4,0},{8,12},{12,8},{1,5},{5,1},{9,13},{13,9},{2,6},{6,2},{1... | collective-permute-start | bytes 1179656 | tf_op jit(solution)/shard_map/ppermute | solution.py:465
  61.5 4.5 %collective-permute-start.10 = (bf16[384,512]{1,0:T(8,128)(2,1)S(1)}, bf16[384,512]{1,0:T(8,128)(2,1)S(1)}, u32[]{:S(2)}, u32[]{:S(2)}) collective-permute-start(bf16[384,512]{1,0:T(8,128)(2,1)S(1)} %shard_map.86.refs_5_), channel_id=1, source_target_pairs={{0,4},{4,0},{8,12},{12,8},{1,5},{5,1},{9,13},{13,9},{2,6},{6,2},{1... | collective-permute-start | bytes 1179656 | tf_op jit(solution)/shard_map/ppermute | solution.py:465
  61.5 4.5 %collective-permute-start.9 = (bf16[384,512]{1,0:T(8,128)(2,1)}, bf16[384,512]{1,0:T(8,128)(2,1)S(1)}, u32[]{:S(2)}, u32[]{:S(2)}) collective-permute-start(bf16[384,512]{1,0:T(8,128)(2,1)} %collective-permute-done.8.refs_3_), channel_id=1, source_target_pairs={{0,4},{4,0},{8,12},{12,8},{1,5},{5,1},{9,13},{13,9},{2,6},{6,2},{1... | collective-permute-start | bytes 1179656 | tf_op jit(solution)/shard_map/ppermute | solution.py:466
  66.0 1.7 %collective-permute-start.12 = (bf16[384,512]{1,0:T(8,128)(2,1)S(1)}, bf16[384,512]{1,0:T(8,128)(2,1)S(1)}, u32[]{:S(2)}, u32[]{:S(2)}) collective-permute-start(bf16[384,512]{1,0:T(8,128)(2,1)S(1)} %collective-permute-done.11.refs_7_), channel_id=1, source_target_pairs={{0,4},{4,0},{8,12},{12,8},{1,5},{5,1},{9,13},{13,9},{2,6},{6,2},{1... | collective-permute-start | bytes 1179656 | tf_op jit(solution)/shard_map/ppermute | solution.py:466
  69.0 18.5 %collective-permute-start.14 = (bf16[768,512]{1,0:T(8,128)(2,1)S(1)}, bf16[768,512]{1,0:T(8,128)(2,1)S(1)}, u32[]{:S(2)}, u32[]{:S(2)}) collective-permute-start(bf16[768,512]{1,0:T(8,128)(2,1)S(1)} %get-tuple-element.66), channel_id=1, source_target_pairs={{0,1},{4,5},{8,9},{12,13},{16,17},{20,21},{24,25},{28,29}} | collective-permute-start | bytes 2359304 | tf_op jit(solution)/shard_map/ppermute | solution.py:454
  69.7 22.3 %collective-permute-start.15 = (bf16[768,512]{1,0:T(8,128)(2,1)S(1)}, bf16[768,512]{1,0:T(8,128)(2,1)S(1)}, u32[]{:S(2)}, u32[]{:S(2)}) collective-permute-start(bf16[768,512]{1,0:T(8,128)(2,1)S(1)} %get-tuple-element.67), channel_id=1, source_target_pairs={{3,2},{7,6},{11,10},{15,14},{19,18},{23,22},{27,26},{31,30}} | collective-permute-start | bytes 2359304 | tf_op jit(solution)/shard_map/ppermute | solution.py:455
  71.0 30.1 %collective-permute-start.16 = (bf16[512,1024]{1,0:T(8,128)(2,1)S(1)}, bf16[512,1024]{1,0:T(8,128)(2,1)S(1)}, u32[]{:S(2)}, u32[]{:S(2)}) collective-permute-start(bf16[512,1024]{1,0:T(8,128)(2,1)S(1)} %copy-done.2), channel_id=1, source_target_pairs={{0,16},{16,0},{1,17},{17,1},{2,18},{18,2},{3,19},{19,3},{4,20},{20... | collective-permute-start | bytes 3145736 | tf_op jit(solution)/shard_map/ppermute | solution.py:443
  81.5 20.3 %collective-permute-start.17 = (bf16[768,512]{1,0:T(8,128)(2,1)S(1)}, bf16[768,512]{1,0:T(8,128)(2,1)S(1)}, u32[]{:S(2)}, u32[]{:S(2)}) collective-permute-start(bf16[768,512]{1,0:T(8,128)(2,1)S(1)} %get-tuple-element.70), channel_id=1, source_target_pairs={{0,1},{1,2},{4,5},{5,6},{8,9},{9,10},{12,13},{13,14},{16,17},{17,1... | collective-permute-start | bytes 2359304 | tf_op jit(solution)/shard_map/ppermute | solution.py:454
  82.8 18.3 %copy-start.12 = (bf16[512,1024]{1,0:T(8,128)(2,1)S(1)}, bf16[512,1024]{1,0:T(8,128)(2,1)}, u32[]{:S(2)}) copy-start(bf16[512,1024]{1,0:T(8,128)(2,1)} %get-tuple-element.83.refs_5_.refs_9_) | copy-start | bytes 3145732
  82.8 26.0 %collective-permute-start.18 = (bf16[768,512]{1,0:T(8,128)(2,1)S(1)}, bf16[768,512]{1,0:T(8,128)(2,1)S(1)}, u32[]{:S(2)}, u32[]{:S(2)}) collective-permute-start(bf16[768,512]{1,0:T(8,128)(2,1)S(1)} %get-tuple-element.71), channel_id=1, source_target_pairs={{2,1},{3,2},{6,5},{7,6},{10,9},{11,10},{14,13},{15,14},{18,17},{19... | collective-permute-start | bytes 2359304 | tf_op jit(solution)/shard_map/ppermute | solution.py:455
  95.3 26.2 %collective-permute-start.19 = (bf16[768,512]{1,0:T(8,128)(2,1)S(1)}, bf16[768,512]{1,0:T(8,128)(2,1)S(1)}, u32[]{:S(2)}, u32[]{:S(2)}) collective-permute-start(bf16[768,512]{1,0:T(8,128)(2,1)S(1)} %get-tuple-element.73), channel_id=1, source_target_pairs={{0,1},{1,2},{4,5},{5,6},{8,9},{9,10},{12,13},{13,14},{16,17},{17,1... | collective-permute-start | bytes 2359304 | tf_op jit(solution)/shard_map/ppermute | solution.py:454
  96.6 29.1 %collective-permute-start.20 = (bf16[768,512]{1,0:T(8,128)(2,1)S(1)}, bf16[768,512]{1,0:T(8,128)(2,1)S(1)}, u32[]{:S(2)}, u32[]{:S(2)}) collective-permute-start(bf16[768,512]{1,0:T(8,128)(2,1)S(1)} %get-tuple-element.74), channel_id=1, source_target_pairs={{2,1},{3,2},{6,5},{7,6},{10,9},{11,10},{14,13},{15,14},{18,17},{19... | collective-permute-start | bytes 2359304 | tf_op jit(solution)/shard_map/ppermute | solution.py:455
  101.2 36.1 %collective-permute-start.21 = (bf16[512,1024]{1,0:T(8,128)(2,1)S(1)}, bf16[512,1024]{1,0:T(8,128)(2,1)S(1)}, u32[]{:S(2)}, u32[]{:S(2)}) collective-permute-start(bf16[512,1024]{1,0:T(8,128)(2,1)S(1)} %copy-done.12), channel_id=1, source_target_pairs={{0,16},{16,0},{1,17},{17,1},{2,18},{18,2},{3,19},{19,3},{4,20},{20... | collective-permute-start | bytes 3145736 | tf_op jit(solution)/shard_map/ppermute | solution.py:443
  115.4 21.9 %collective-permute-start.22 = (bf16[768,512]{1,0:T(8,128)(2,1)S(1)}, bf16[768,512]{1,0:T(8,128)(2,1)S(1)}, u32[]{:S(2)}, u32[]{:S(2)}) collective-permute-start(bf16[768,512]{1,0:T(8,128)(2,1)S(1)} %get-tuple-element.77), channel_id=1, source_target_pairs={{0,1},{1,2},{2,3},{4,5},{5,6},{6,7},{8,9},{9,10},{10,11},{12,13},{... | collective-permute-start | bytes 2359304 | tf_op jit(solution)/shard_map/ppermute | solution.py:454
  117.6 25.0 %collective-permute-start.23 = (bf16[768,512]{1,0:T(8,128)(2,1)S(1)}, bf16[768,512]{1,0:T(8,128)(2,1)S(1)}, u32[]{:S(2)}, u32[]{:S(2)}) collective-permute-start(bf16[768,512]{1,0:T(8,128)(2,1)S(1)} %get-tuple-element.78), channel_id=1, source_target_pairs={{1,0},{2,1},{3,2},{5,4},{6,5},{7,6},{9,8},{10,9},{11,10},{13,12},{... | collective-permute-start | bytes 2359304 | tf_op jit(solution)/shard_map/ppermute | solution.py:455
  131.3 20.7 %collective-permute-start.24 = (bf16[768,512]{1,0:T(8,128)(2,1)S(1)}, bf16[768,512]{1,0:T(8,128)(2,1)S(1)}, u32[]{:S(2)}, u32[]{:S(2)}) collective-permute-start(bf16[768,512]{1,0:T(8,128)(2,1)S(1)} %get-tuple-element.80), channel_id=1, source_target_pairs={{0,1},{1,2},{2,3},{4,5},{5,6},{6,7},{8,9},{9,10},{10,11},{12,13},{... | collective-permute-start | bytes 2359304 | tf_op jit(solution)/shard_map/ppermute | solution.py:454
  133.2 25.4 %collective-permute-start.25 = (bf16[768,512]{1,0:T(8,128)(2,1)S(1)}, bf16[768,512]{1,0:T(8,128)(2,1)S(1)}, u32[]{:S(2)}, u32[]{:S(2)}) collective-permute-start(bf16[768,512]{1,0:T(8,128)(2,1)S(1)} %get-tuple-element.81), channel_id=1, source_target_pairs={{1,0},{2,1},{3,2},{5,4},{6,5},{7,6},{9,8},{10,9},{11,10},{13,12},{... | collective-permute-start | bytes 2359304 | tf_op jit(solution)/shard_map/ppermute | solution.py:455
  (16 other events, 163.2 us)
